TPU v7x, 32 devices: a whole 2x2x4 slice. The times are simulated.
32 devices in a mesh: wafer: 4 (over y, x), span: 8 (over z, core).
Axes of the slice: x: 2, y: 2, z: 4, core: 2. Of those that a mesh axis runs over, the one named last changes fastest.
Arguments:
- timestream: float32 [192, 2048], P(('wafer', 'span')), may hold values from -6 to 6
- templates: float32 [64, 2048], P(None, 'span'), may hold values from -0.125 to 0.125
- bias_group: int32 [192], P('wafer'), may hold values from 0 to 11, as said below
- det_weight: float32 [192], P('wafer'), may hold values from 0.2 to 5
- cut_start: int32 [192], P('wafer'), may hold values from 0 to 2047
- cut_len: int32 [192], P('wafer'), may hold values from 1 to 511
- pointing: int32 [192, 2048], P('wafer', 'span'), may hold values from 0 to 4095
- hit_tiles: int32 [8, 8], replicated, may hold values from 0 to 63, as said below
Outputs:
- fit_coeffs: float32 [192, 64], P(('wafer', 'span'))
- rhs_map: float32 [64, 512], P('span', 'wafer')
- weight_map: float32 [64, 512], P('span', 'wafer')
Inputs may be any that keep to these rules, and one draw needn't show every extreme that they name: `bias_group`: within each wafer's 48 detectors every bias line holds exactly 4 detectors. `hit_tiles`: each row lists distinct tiles; tile t is owned by index t // 8 of span; every row holds exactly 2 tiles of each owner it names: of one owner common to all rows, and of 3 other owners.
All inputs are finite; a program needn't handle non-finite values.
Results may differ from a plain program's by a relative error of at most 0.0041.
Values sent between devices are 32-bit elements; how exact they have to be, the bound alone decides.
A program may use at most 64 MiB of HBM per device.

v0:
```python
import math

import jax
import jax.numpy as jnp
from jax import lax
from jax.sharding import PartitionSpec as P

NGROUP = 12
TILE = 512
TILE_OWN = 8
CAP = 2


def solve_normal(matrix, right_side):
    factor = jnp.linalg.cholesky(matrix)
    middle = lax.linalg.triangular_solve(factor, right_side, left_side=True, lower=True)
    return lax.linalg.triangular_solve(factor, middle, left_side=True, lower=True, transpose_a=True)


def bin_samples(weighted, sample_weight, pointing, tiles_listed):
    rows = weighted.shape[0]
    block_dets = math.gcd(rows, 64)
    block_count = rows // block_dets
    fine_width = min(128, TILE)
    coarse_width = tiles_listed * TILE // fine_width
    blocks = (
        weighted.reshape(block_count, -1),
        sample_weight.reshape(block_count, -1),
        pointing.reshape(block_count, -1),
    )
    zero_value = jnp.zeros((), jnp.bfloat16)

    def accumulate(totals, block_data):
        values_block, weights_block, points_block = block_data
        coarse_index = points_block // fine_width
        fine_index = points_block % fine_width
        coarse_hot = coarse_index[None, :] == jnp.arange(coarse_width, dtype=jnp.int32)[:, None]
        left_hot = jnp.concatenate(
            [
                jnp.where(coarse_hot, values_block[None, :], zero_value),
                jnp.where(coarse_hot, weights_block[None, :], zero_value),
            ],
            axis=0,
        )
        right_hot = (
            fine_index[None, :] == jnp.arange(fine_width, dtype=jnp.int32)[:, None]
        ).astype(jnp.bfloat16)
        product = lax.dot_general(
            left_hot, right_hot, (((1,), (1,)), ((), ())), preferred_element_type=jnp.float32
        )
        return (totals + product, None)

    totals, unused = lax.scan(
        accumulate, jnp.zeros((2 * coarse_width, fine_width), jnp.float32), blocks
    )
    return totals.reshape(2, tiles_listed, TILE)


def body(timestream, templates, bias_group, det_weight, cut_start, cut_len, pointing, hit_tiles):
    highest = lax.Precision.HIGHEST
    spans = lax.axis_size("span")
    own_index = lax.axis_index("span")
    det_dev = timestream.shape[0]
    span_len = templates.shape[1]
    det_wafer = det_dev * spans
    line_scale = NGROUP / det_wafer
    groups = lax.dynamic_slice_in_dim(bias_group, own_index * det_dev, det_dev)
    onehot = (groups[None, :] == jnp.arange(NGROUP, dtype=jnp.int32)[:, None]).astype(jnp.float32)
    line_sums = lax.psum(
        jnp.dot(onehot, timestream, precision=highest, preferred_element_type=jnp.float32), "span"
    )
    cleaned = timestream - jnp.dot(
        onehot.T, line_sums * line_scale, precision=highest, preferred_element_type=jnp.float32
    )
    all_templates = lax.all_gather(templates, "span", axis=1, tiled=True)
    normal_matrix = jnp.dot(
        all_templates, all_templates.T, precision=highest, preferred_element_type=jnp.float32
    )
    projection = jnp.dot(
        all_templates, cleaned.T, precision=highest, preferred_element_type=jnp.float32
    )
    amplitudes = solve_normal(normal_matrix, projection)
    fit_coeffs = amplitudes.T
    outgoing = cleaned - jnp.dot(
        amplitudes.T, all_templates, precision=highest, preferred_element_type=jnp.float32
    )
    regrouped = lax.all_to_all(outgoing, "span", split_axis=1, concat_axis=0, tiled=True)
    sample_time = own_index * span_len + jnp.arange(span_len, dtype=jnp.int32)
    inside = (sample_time[None, :] >= cut_start[:, None]) & (
        sample_time[None, :] < (cut_start + cut_len)[:, None]
    )
    sample_weight = jnp.where(inside, jnp.float32(0.0), det_weight[:, None]).astype(jnp.bfloat16)
    weighted = (sample_weight.astype(jnp.float32) * regrouped).astype(jnp.bfloat16)
    tiles_listed = hit_tiles.shape[1]
    partial_value = bin_samples(weighted, sample_weight, pointing, tiles_listed)
    shared = lax.psum_scatter(partial_value, "wafer", scatter_dimension=2, tiled=True)
    owners = hit_tiles // TILE_OWN
    earlier = jnp.arange(tiles_listed)[:, None] > jnp.arange(tiles_listed)[None, :]
    same_owner = owners[:, :, None] == owners[:, None, :]
    slot_rank = jnp.sum((same_owner & earlier[None, :, :]).astype(jnp.int32), axis=2)
    own_owners = lax.dynamic_index_in_dim(owners, own_index, 0, keepdims=False)
    own_rank = lax.dynamic_index_in_dim(slot_rank, own_index, 0, keepdims=False)
    to_owner = own_owners[None, None, :] == jnp.arange(spans, dtype=jnp.int32)[:, None, None]
    to_slot = own_rank[None, None, :] == jnp.arange(CAP, dtype=jnp.int32)[None, :, None]
    selector = (to_owner & to_slot).astype(jnp.float32)
    outbox = jnp.einsum("oks,jsp->okjp", selector, shared, precision=highest)
    received = lax.all_to_all(outbox, "span", split_axis=0, concat_axis=0, tiled=True)
    for_me = (owners == own_index)[:, :, None]
    slot_hot = (
        (slot_rank[:, :, None] == jnp.arange(CAP, dtype=jnp.int32)[None, None, :]) & for_me
    ).astype(jnp.float32)
    tile_hot = (
        (hit_tiles - own_index * TILE_OWN)[:, :, None]
        == jnp.arange(TILE_OWN, dtype=jnp.int32)[None, None, :]
    ).astype(jnp.float32)
    arrival = jnp.einsum("csk,csj->ckj", slot_hot, tile_hot, precision=highest)
    owned_tiles = jnp.einsum("ckj,ckrp->jrp", arrival, received, precision=highest)
    return (fit_coeffs, owned_tiles[:, 0, :], owned_tiles[:, 1, :])


def solution(mesh):
    in_specs = (
        P(("wafer", "span"), None),
        P(None, "span"),
        P("wafer"),
        P("wafer"),
        P("wafer"),
        P("wafer"),
        P("wafer", "span"),
        P(),
    )
    out_specs = (P(("wafer", "span"), None), P("span", "wafer"), P("span", "wafer"))
    return jax.shard_map(body, mesh=mesh, in_specs=in_specs, out_specs=out_specs, check_vma=False)
```

profile of v0, /device:TPU:0, one launch (start us, length us, event | category | flops | bytes accessed | tf_op | source)
XLA Modules:
  0.0 123.6 jit_solution(708048436743447176)
XLA Ops:
  7.2 0.7 dynamic_slice.32
  7.9 1.7 %fusion.24 = f32[12,2048]{1,0:T(8,128)} fusion(f32[6,2048]{1,0:T(8,128)} %param.10, s32[6]{0:T(128)S(1)} %dynamic_slice.32), kind=kOutput, calls=%fused_computation.51 | convolution fusion | flops 1769544 | bytes 147480 | tf_op jit(solution)/shard_map/dot_general | solution.py:70
  9.6 16.8 %all_gather.3 = f32[64,2048]{1,0:T(8,128)S(1)} all-gather(f32[64,256]{1,0:T(8,128)} %param.11), channel_id=1, replica_groups=mesh['wafer'=4,'span'=8] {'span'}, dimensions={1}, use_global_device_ids=true | all-gather | bytes 589824 | tf_op jit(solution)/shard_map/all_gather | solution.py:75
  26.4 0.6 fusion.36
  27.1 5.8 %cholesky.16 = f32[64,64]{1,0:T(8,128)S(1)} custom-call(f32[64,64]{1,0:T(8,128)S(1)} %fusion.16), custom_call_target="Cholesky" | custom-call | tf_op jit(solution)/shard_map/jit(cholesky)/cholesky | solution.py:15
  33.0 0.6 compare_reduce_fusion
  33.7 0.7 fusion.11
  34.9 0.3 convert_reduce_fusion
  35.2 4.9 %custom-call.8 = f32[1,64,64]{1,2,0:T(8,128)S(1)} custom-call(f32[1,64,64]{2,1,0:T(8,128)S(1)} %fusion.11), custom_call_target="InvertDiagBlocksLowerTriangular" | custom-call | tf_op jit(solution)/shard_map/triangular_solve | solution.py:17
  40.3 27.3 %all-reduce.2.cloned.1.call-done = f32[12,2048]{1,0:T(8,128)} async-done(((f32[12,2048]{1,0:T(8,128)}), f32[12,2048]{1,0:T(8,128)}) %all-reduce.2.cloned.1.call-update) | async-done | bytes 98320 | tf_op jit(solution)/shard_map/psum | solution.py:69
  67.6 1.1 convolution_subtract_fusion.1
  68.7 0.5 fusion.37
  69.2 0.2 fusion.14
  69.4 0.2 fusion.12
  69.5 1.0 convolution_subtract_fusion
  70.5 3.3 %all-to-all-start = ((f32[6,8,256]{2,0,1:T(8,128)}), f32[6,8,256]{2,0,1:T(8,128)S(1)}, u32[]{:S(2)}, u32[]{:S(2)}) async-start(f32[6,8,256]{2,0,1:T(8,128)} %bitcast.9), calls=%async_computation | async-start | bytes 131072 | tf_op jit(solution)/shard_map/all_to_all | solution.py:87
  74.0 5.8 %all-to-all-done = f32[6,8,256]{2,0,1:T(8,128)S(1)} async-done(((f32[6,8,256]{2,0,1:T(8,128)}), f32[6,8,256]{2,0,1:T(8,128)S(1)}, u32[]{:S(2)}, u32[]{:S(2)}) %all-to-all-start) | async-done | bytes 49184 | tf_op jit(solution)/shard_map/all_to_all | solution.py:87
  79.8 2.7 %while.13 = (s32[]{:T(128)}, f32[64,128]{1,0:T(8,128)S(1)}, s32[3,4096]{1,0:T(4,128)S(1)}, bf16[3,4096]{1,0:T(4,128)(2,1)S(1)}, bf16[3,4096]{1,0:T(4,128)(2,1)S(1)}, /*index=5*/s32[]{:T(128)}, s32[]{:T(128)}) while((s32[]{:T(128)}, f32[64,128]{1,0:T(8,128)S(1)}, s32[3,4096]{1,0:T(4,128)S(1)}, bf16[3,4096]{1,0:T(4,128)(2,1)S(1)}, ...), condition=%wide.region_5.6_spmd.clone, body=%wide.region_4.5_spmd.clone.sunk | while | flops 69173248 | bytes 1278047 | solution.py:53
  79.9 0.1 dynamic-slice_reduce_fusion.3
  80.2 0.6 fusion.52
  80.8 0.1 dynamic-slice_reduce_fusion.3
  81.1 0.5 fusion.52
  82.0 0.5 fusion.52
  82.6 0.6 reshape.126
  83.2 21.1 %reduce-scatter.2.cloned.1.call-done = f32[2,8,128]{2,1,0:T(8,128)} async-done(((f32[2,8,512]{2,1,0:T(8,128)}), f32[2,8,128]{2,1,0:T(8,128)}) %reduce-scatter.2.cloned.1.call-update) | async-done | bytes 8208 | tf_op jit(solution)/shard_map/reduce_scatter | solution.py:96
  104.3 0.8 fusion.20
  105.1 0.6 copy.22
  105.7 4.6 %all-to-all-start.1 = ((f32[8,2,2,128]{3,1,2,0:T(2,128)}), f32[8,2,2,128]{3,1,2,0:T(2,128)S(1)}, u32[]{:S(2)}, u32[]{:S(2)}) async-start(f32[8,2,2,128]{3,1,2,0:T(2,128)} %copy.22), calls=%async_computation.2 | async-start | bytes 32768 | tf_op jit(solution)/shard_map/all_to_all | solution.py:107
  110.3 0.2 fusion.17
  110.5 5.4 %all-to-all-done.1 = f32[8,2,2,128]{3,1,2,0:T(2,128)S(1)} async-done(((f32[8,2,2,128]{3,1,2,0:T(2,128)}), f32[8,2,2,128]{3,1,2,0:T(2,128)S(1)}, u32[]{:S(2)}, u32[]{:S(2)}) %all-to-all-start.1) | async-done | bytes 16416 | tf_op jit(solution)/shard_map/all_to_all | solution.py:107
  115.9 0.2 convolution_bitcast_fusion
  116.1 0.6 slice_bitcast_fusion
  (55 shorter events, 1.8 us)
Async XLA Ops:
  7.2 60.4 %all-reduce.2.cloned.1.call-start = ((), (), s32[]{:S(2)}) async-start(), calls=%async_computation.3 | async-start | bytes 262144 | tf_op jit(solution)/shard_map/psum | solution.py:69
  26.4 7.9 %copy-start.4 = (s32[48]{0:T(128)S(1)}, s32[48]{0:T(128)}, u32[]{:S(2)}) copy-start(s32[48]{0:T(128)} %param.14) | copy-start | bytes 580
  26.4 8.0 %copy-start.5 = (s32[48]{0:T(128)S(1)}, s32[48]{0:T(128)}, u32[]{:S(2)}) copy-start(s32[48]{0:T(128)} %param.15) | copy-start | bytes 580
  26.4 8.2 %copy-start.6 = (f32[48]{0:T(128)S(1)}, f32[48]{0:T(128)}, u32[]{:S(2)}) copy-start(f32[48]{0:T(128)} %param.13) | copy-start | bytes 580
  26.4 8.4 %copy-start.3 = (s32[8,8]{1,0:T(8,128)S(1)}, s32[8,8]{1,0:T(8,128)}, u32[]{:S(2)}) copy-start(s32[8,8]{1,0:T(8,128)} %param.17) | copy-start | bytes 772
  27.0 13.2 %copy-start.1 = (s32[48,256]{1,0:T(8,128)S(1)}, s32[48,256]{1,0:T(8,128)}, u32[]{:S(2)}) copy-start(s32[48,256]{1,0:T(8,128)} %param.16) | copy-start | bytes 147460
  27.0 40.5 %copy-start = (f32[6,2048]{1,0:T(8,128)S(1)}, f32[6,2048]{1,0:T(8,128)}, u32[]{:S(2)}) copy-start(f32[6,2048]{1,0:T(8,128)} %param.10) | copy-start | bytes 147460
  69.5 10.3 %copy-start.2 = (f32[64,6]{0,1:T(8,128)}, f32[64,6]{0,1:T(8,128)S(1)}, u32[]{:S(2)}) copy-start(f32[64,6]{0,1:T(8,128)S(1)} %fusion.12) | copy-start | bytes 4612
  70.5 9.2 %all-to-all-start = ((f32[6,8,256]{2,0,1:T(8,128)}), f32[6,8,256]{2,0,1:T(8,128)S(1)}, u32[]{:S(2)}, u32[]{:S(2)}) async-start(f32[6,8,256]{2,0,1:T(8,128)} %bitcast.9), calls=%async_computation | async-start | bytes 131072 | tf_op jit(solution)/shard_map/all_to_all | solution.py:87
  73.9 30.4 %reduce-scatter.2.cloned.1.call-start = ((), (), s32[]{:S(2)}) async-start(), calls=%async_computation.4 | async-start | bytes 40960 | tf_op jit(solution)/shard_map/reduce_scatter | solution.py:96
  105.7 10.2 %all-to-all-start.1 = ((f32[8,2,2,128]{3,1,2,0:T(2,128)}), f32[8,2,2,128]{3,1,2,0:T(2,128)S(1)}, u32[]{:S(2)}, u32[]{:S(2)}) async-start(f32[8,2,2,128]{3,1,2,0:T(2,128)} %copy.22), calls=%async_computation.2 | async-start | bytes 32768 | tf_op jit(solution)/shard_map/all_to_all | solution.py:107
Sparse Core Ops, SparseCore 0:
  10.3 57.1 all-reduce.1
  83.3 20.9 reduce-scatter.1
where the time goes:
time: 124 us
  waiting for transfers between devices  59.5 us (48%)
  blocking collectives  16.8 us (14%)
  between operations  14.3 us (12%)
  other arithmetic  13.1 us (11%)
  matrix products  8.04 us (6%)
  starting transfers between devices  8.01 us (6%)
  local copies, waits for them, and re-layouts  3.73 us (3%)
    psum x1, waiting for transfers between devices, body(): lax.psum(jnp.dot(onehot, timestream, precision=highest, preferred_element...  27.3 us
    reduce_scatter x1, waiting for transfers between devices, body(): lax.psum_scatter(partial_value, 'wafer', scatter_dimension=2, tiled=True)  21.1 us
    all_gather x1, blocking collectives, body(): all_templates = lax.all_gather(templates, 'span', axis=1, tiled=True)  16.8 us
    another operation x3, other arithmetic, solve_normal(): factor = jnp.linalg.cholesky(matrix)  6.52 us
    all_to_all x1, waiting for transfers between devices, body(): lax.all_to_all(outgoing, 'span', split_axis=1, concat_axis=0, tiled=True)  5.78 us
    another operation x2, other arithmetic, solve_normal(): lax.linalg.triangular_solve(factor, middle, left_side=True, lower=True, t...  5.57 us
    all_to_all x1, waiting for transfers between devices, body(): lax.all_to_all(outbox, 'span', split_axis=0, concat_axis=0, tiled=True)  5.38 us
    all_to_all x1, starting transfers between devices, body(): lax.all_to_all(outbox, 'span', split_axis=0, concat_axis=0, tiled=True)  4.58 us
  transfers between devices with their start and end apart: 4, of which 4 were waited for; matrix products, arithmetic and copies ran while one was open for 11% of the time, Pallas kernels for 0%

commit v1 on v0

v1 whole, which is shorter than its diff:
```python
import functools

import jax
import jax.numpy as jnp
from jax import lax
from jax.experimental import pallas as pl
from jax.experimental.pallas import tpu as pltpu
from jax.sharding import PartitionSpec as P

NGROUP = 12
TILE = 512
TILE_OWN = 8
CAP = 2
ROWS = 8
HIGHEST = lax.Precision.HIGHEST
MESH = pl.DeviceIdType.MESH
F32 = jnp.float32
BF16 = jnp.bfloat16


def dot_nn(a, b):
    return lax.dot_general(a, b, (((1,), (0,)), ((), ())), precision=HIGHEST, preferred_element_type=F32)


def dot_nt(a, b):
    return lax.dot_general(a, b, (((1,), (1,)), ((), ())), precision=HIGHEST, preferred_element_type=F32)


def dot_tn(a, b):
    return lax.dot_general(a, b, (((0,), (0,)), ((), ())), precision=HIGHEST, preferred_element_type=F32)


def iota(shape, dim):
    return lax.broadcasted_iota(jnp.int32, shape, dim)


def to_column(row):
    size = row.shape[1]
    eye = iota((size, size), 0) == iota((size, size), 1)
    return jnp.sum(jnp.where(eye, row.astype(F32), 0.0), axis=1, keepdims=True)


def log2(value):
    assert value & (value - 1) == 0
    return value.bit_length() - 1


def inverse_spd(gram):
    size = gram.shape[0]
    eye = (iota((size, size), 0) == iota((size, size), 1)).astype(F32)
    wide = jnp.concatenate([eye, gram], axis=1)
    blocks = [wide[ROWS * b : ROWS * (b + 1), :] for b in range(size // ROWS)]
    below = iota((ROWS, 1), 0)
    for k in range(size):
        first, r = k // ROWS, k % ROWS
        row = blocks[first][r : r + 1, :]
        scaled = row * (1.0 / row[:, size + k : size + k + 1])
        for b in range(first, len(blocks)):
            if b == first and r == ROWS - 1:
                continue
            column = blocks[b][:, size + k : size + k + 1]
            if b == first:
                column = jnp.where(below > r, column, 0.0)
            blocks[b] = blocks[b] - column * scaled
    done = jnp.concatenate(blocks, axis=0)
    on_diag = iota(done.shape, 0) + size == iota(done.shape, 1)
    pivots = jnp.sum(jnp.where(on_diag, done, 0.0), axis=1, keepdims=True)
    lower = done[:, :size]
    return dot_tn(lower, lower / pivots)


def kernel(
    wafers, spans,
    ts_ref, tm_ref, bg_ref, dw_ref, cs_ref, cl_ref, pt_ref, ht_ref,
    fit_ref, rhs_ref, wgt_ref,
    ts_rx, ts_all, gr_rx, pj_rx, sw_ref, val_ref, hot_ref, tx, rx,
    span_send, span_recv, tile_send, tile_recv,
):
    det_dev = ts_ref.shape[0]
    nt, span_len = tm_ref.shape
    det_w = pt_ref.shape[0]
    hits = ht_ref.shape[1]
    total = wafers * spans
    pix = TILE // wafers
    my_w, my_s = lax.axis_index("wafer"), lax.axis_index("span")
    me = my_w * spans + my_s

    def peer(i):
        other = lax.rem(me + i, total)
        return other, lax.div(other, spans), lax.rem(other, spans)

    barrier = pltpu.get_barrier_semaphore()

    def greet(i, carry):
        unused, w, s = peer(i)
        pl.semaphore_signal(barrier, inc=1, device_id=(w, s), device_id_type=MESH)
        return carry

    lax.fori_loop(1, total, greet, 0)

    templates = tm_ref[...]
    gr_rx[my_s] = dot_nt(templates, templates)
    ts_rx[my_s] = ts_ref[:, pl.ds(pl.multiple_of(my_s * span_len, span_len), span_len)]
    pl.semaphore_wait(barrier, total - 1)

    def to_span(src, dst, which, s):
        pltpu.make_async_remote_copy(
            src_ref=src, dst_ref=dst, send_sem=span_send.at[which], recv_sem=span_recv.at[which],
            device_id=(my_w, s), device_id_type=MESH,
        ).start()

    def span_wait(buffer, sems, which):
        slots = buffer.at[pl.ds(0, spans - 1)]
        pltpu.make_async_copy(slots, slots, sems.at[which]).wait()

    others = [lax.rem(my_s + i, spans) for i in range(1, spans)]
    for s in others:
        start = pl.multiple_of(s * span_len, span_len)
        to_span(ts_ref.at[:, pl.ds(start, span_len)], ts_rx.at[my_s], 0, s)
    for s in others:
        to_span(gr_rx.at[my_s], gr_rx.at[my_s], 1, s)

    listed = ht_ref[...]
    owner = lax.shift_right_logical(listed, jnp.full(listed.shape, log2(TILE_OWN), jnp.int32)).astype(F32)
    lane = iota(listed.shape, 1)
    rank = jnp.zeros(listed.shape, F32)
    for j in range(hits - 1):
        rank += jnp.where((owner[:, j : j + 1] == owner) & (lane > j), 1.0, 0.0)
    code = owner * CAP + rank
    own_code = jnp.sum(jnp.where(iota(listed.shape, 0) == my_s, code, 0.0), axis=0, keepdims=True)
    slots = spans * CAP
    selector = (own_code == iota((slots, hits), 0).astype(F32)).astype(F32)
    landing = []
    for k in range(CAP):
        mine = code == (my_s * CAP + k).astype(F32)
        place = (listed - (my_s * TILE_OWN - 1)).astype(F32)
        landing.append(jnp.sum(jnp.where(mine, place, 0.0), axis=1, keepdims=True) - 1.0)

    time = (iota((det_w, span_len), 1) + my_s * span_len).astype(F32)
    cut_start = to_column(cs_ref[...])
    cut_end = cut_start + to_column(cl_ref[...])
    inside = (time >= cut_start) & (time < cut_end)
    sw_ref[...] = jnp.where(inside, 0.0, to_column(dw_ref[...])).astype(BF16).astype(F32)

    coarse_count = wafers * hits
    coarse_iota = iota((coarse_count, span_len), 0)
    fine_iota = iota((pix, span_len), 0)

    def shifted(x, amount):
        return lax.shift_right_logical(x, jnp.full(x.shape, amount, jnp.int32))

    def coarse_of(points):
        return (shifted(points, log2(pix)) & (wafers - 1)) * hits + shifted(points, log2(TILE))

    def bin_rows(source, first_time):
        def step(g, acc):
            rows = pl.ds(pl.multiple_of(g * ROWS, ROWS), ROWS)
            points = pt_ref[rows, :]
            coarse = coarse_of(points)
            fine = points & (pix - 1)
            values = source[rows, :]
            for r in range(ROWS):
                left = jnp.where(coarse_iota == coarse[r : r + 1, :], values[r : r + 1, :], 0.0).astype(BF16)
                if first_time:
                    right = jnp.where(fine_iota == fine[r : r + 1, :], 1.0, 0.0).astype(BF16)
                    hot_ref[g * ROWS + r] = right
                else:
                    right = hot_ref[g * ROWS + r]
                acc = acc + lax.dot_general(
                    left, right, (((1,), (1,)), ((), ())), preferred_element_type=F32
                )
            return acc

        return lax.fori_loop(0, det_w // ROWS, step, jnp.zeros((coarse_count, pix), F32))

    def send_tiles(part, m):
        wide = jnp.concatenate([part[q * hits : (q + 1) * hits, :] for q in range(wafers)], axis=1)
        out = dot_nn(selector, wide)
        for q in range(wafers):
            for o in range(spans):
                tx[m, q * spans + o] = out[o * CAP : (o + 1) * CAP, q * pix : (q + 1) * pix]
        rx[m, me] = tx[m, me]

        def send(i, carry):
            other, w, s = peer(i)
            pltpu.make_async_remote_copy(
                src_ref=tx.at[m, other], dst_ref=rx.at[m, me],
                send_sem=tile_send.at[m], recv_sem=tile_recv.at[m],
                device_id=(w, s), device_id_type=MESH,
            ).start()
            return carry

        lax.fori_loop(1, total, send, 0)

    def tile_wait(buffer, sems, m):
        part = buffer.at[m, pl.ds(0, total - 1)]
        pltpu.make_async_copy(part, part, sems.at[m]).wait()

    def collect(m):
        row_iota = iota((TILE_OWN, pix), 0).astype(F32)
        acc = jnp.zeros((TILE_OWN, pix), F32)
        for s in range(spans):
            arrived = rx[m, s]
            for w in range(1, wafers):
                arrived = arrived + rx[m, w * spans + s]
            for k in range(CAP):
                acc = acc + jnp.where(row_iota == landing[k][s : s + 1, :], arrived[k : k + 1, :], 0.0)
        return acc

    send_tiles(bin_rows(sw_ref, True), 1)

    same_line = (bg_ref[...].astype(F32) == to_column(bg_ref[...])).astype(F32)
    span_wait(ts_rx, span_recv, 0)
    for s in range(spans):
        ts_all[s * det_dev : (s + 1) * det_dev, :] = ts_rx[s]
    stream = ts_all[...]
    cleaned = stream - dot_nn(same_line, stream) * (NGROUP / det_w)
    pj_rx[my_s] = dot_nt(cleaned, templates)
    for s in others:
        to_span(pj_rx.at[my_s], pj_rx.at[my_s], 2, s)

    span_wait(gr_rx, span_recv, 1)
    inverse = inverse_spd(jnp.sum(gr_rx[...], axis=0))
    solved = dot_nn(inverse, templates)

    span_wait(pj_rx, span_recv, 2)
    projection = jnp.sum(pj_rx[...], axis=0)
    filtered = cleaned - dot_nn(projection, solved)
    val_ref[...] = (sw_ref[...] * filtered).astype(BF16).astype(F32)
    send_tiles(bin_rows(val_ref, False), 0)

    mine = (iota((det_dev, det_w), 1) == iota((det_dev, det_w), 0) + my_s * det_dev).astype(F32)
    fit_ref[...] = dot_nn(dot_nn(mine, projection), inverse)
    tile_wait(rx, tile_recv, 1)
    wgt_ref[...] = collect(1)
    tile_wait(rx, tile_recv, 0)
    rhs_ref[...] = collect(0)
    for which, buffer in enumerate((ts_rx, gr_rx, pj_rx)):
        span_wait(buffer, span_send, which)
    for m in range(2):
        tile_wait(tx, tile_send, m)


def body(timestream, templates, bias_group, det_weight, cut_start, cut_len, pointing, hit_tiles):
    wafers, spans = lax.axis_size("wafer"), lax.axis_size("span")
    det_dev = timestream.shape[0]
    nt, span_len = templates.shape
    det_w = pointing.shape[0]
    pix = TILE // wafers
    total = wafers * spans
    vmem = pl.BlockSpec(memory_space=pltpu.VMEM)
    return pl.pallas_call(
        functools.partial(kernel, wafers, spans),
        out_shape=(
            jax.ShapeDtypeStruct((det_dev, nt), F32),
            jax.ShapeDtypeStruct((TILE_OWN, pix), F32),
            jax.ShapeDtypeStruct((TILE_OWN, pix), F32),
        ),
        in_specs=[vmem] * 8,
        out_specs=(vmem,) * 3,
        scratch_shapes=[
            pltpu.VMEM((spans, det_dev, span_len), F32),
            pltpu.VMEM((det_w, span_len), F32),
            pltpu.VMEM((spans, nt, nt), F32),
            pltpu.VMEM((spans, det_w, nt), F32),
            pltpu.VMEM((det_w, span_len), F32),
            pltpu.VMEM((det_w, span_len), F32),
            pltpu.VMEM((det_w, pix, span_len), BF16),
            pltpu.VMEM((2, total, CAP, pix), F32),
            pltpu.VMEM((2, total, CAP, pix), F32),
            pltpu.SemaphoreType.DMA((3,)),
            pltpu.SemaphoreType.DMA((3,)),
            pltpu.SemaphoreType.DMA((2,)),
            pltpu.SemaphoreType.DMA((2,)),
        ],
        compiler_params=pltpu.CompilerParams(
            collective_id=0, has_side_effects=True, vmem_limit_bytes=56 * 1024 * 1024
        ),
    )(
        timestream, templates, bias_group.reshape(1, det_w), det_weight.reshape(1, det_w),
        cut_start.reshape(1, det_w), cut_len.reshape(1, det_w), pointing, hit_tiles,
    )


def solution(mesh):
    in_specs = (
        P(("wafer", "span"), None),
        P(None, "span"),
        P("wafer"),
        P("wafer"),
        P("wafer"),
        P("wafer"),
        P("wafer", "span"),
        P(),
    )
    out_specs = (P(("wafer", "span"), None), P("span", "wafer"), P("span", "wafer"))
    return jax.shard_map(body, mesh=mesh, in_specs=in_specs, out_specs=out_specs, check_vma=False)
```

time: 124 us -> 33.2 us (0.27)
  waiting for transfers between devices: 59.5 us -> 0 us
  Pallas kernels: 0 us -> 29.7 us
  blocking collectives: 16.8 us -> 0 us
  between operations: 14.3 us -> 0.65 us
  other arithmetic: 13.1 us -> 0 us
  matrix products: 8.04 us -> 0 us
  starting transfers between devices: 8.01 us -> 0 us
    pallas_call x0 -> x1, Pallas kernels: none -> 29.7 us  [body(): pl.pallas_call(functools.partial(kernel, wafers, spans), out_shape=(jax.S...]
    psum x1 -> x0, waiting for transfers between devices: 27.3 us -> none  [body(): lax.psum(jnp.dot(onehot, timestream, precision=highest, preferred_element...]
    reduce_scatter x1 -> x0, waiting for transfers between devices: 21.1 us -> none  [body(): lax.psum_scatter(partial_value, 'wafer', scatter_dimension=2, tiled=True)]
    all_gather x1 -> x0, blocking collectives: 16.8 us -> none  [body(): all_templates = lax.all_gather(templates, 'span', axis=1, tiled=True)]
    another operation x5 -> x0, other arithmetic: 12.1 us -> none  [the longest x3 6.52 us: solve_normal(): factor = jnp.linalg.cholesky(matrix)]
    all_to_all x2 -> x0, waiting for transfers between devices: 11.2 us -> none  [the longest x1 5.78 us: body(): lax.all_to_all(outgoing, 'span', split_axis=1, concat_axis=0, tiled=True)]
    all_to_all x2 -> x0, starting transfers between devices: 7.93 us -> none  [the longest x1 4.58 us: body(): lax.all_to_all(outbox, 'span', split_axis=0, concat_axis=0, tiled=True)]
    dot_general x11 -> x0, matrix products: 7.73 us -> none  [the longest x1 1.67 us: body(): jnp.dot(onehot, timestream, precision=highest, preferred_element_type=jnp...]
  transfers between devices with their start and end apart: 4 -> 0, of which waited for: 4 -> 0; matrix products, arithmetic and copies ran while one was open for 11% -> 0% of each run, Pallas kernels for 0% -> 0%
where the time goes in v1:
time: 33.2 us; the launch traced here: 32.9 us
  Pallas kernels  29.7 us (89%)
  local copies, waits for them, and re-layouts  2.62 us (8%)
  between operations  0.65 us (2%)
    pallas_call x1, Pallas kernels, body(): pl.pallas_call(functools.partial(kernel, wafers, spans), out_shape=(jax.S...  29.7 us
    unnamed x9, local copies, waits for them, and re-layouts  2.62 us

profile of v1, /device:TPU:0, one launch (start us, length us, event | category | flops | bytes accessed | tf_op | source)
XLA Modules:
  0.0 32.9 jit_solution(11738415900861181061)
XLA Ops:
  0.6 29.7 %shard_map.103 = (f32[6,64]{1,0:T(8,128)}, f32[8,128]{1,0:T(8,128)}, f32[8,128]{1,0:T(8,128)}) custom-call(f32[6,2048]{1,0:T(8,128)} %ts_ref.1, f32[64,256]{1,0:T(8,128)} %tm_ref.1, s32[1,48]{1,0:T(1,128)} %bitcast.4, f32[1,48]{1,0:T(1,128)} %bitcast.5, s32[1,48]{1,0:T(1,128)} %bitcast.6, s32[1,48]{1,0:T(1,128)} %bitcast.7, s32[48,256]{1,0:T(8,128)} %pt_ref.1, ...), custom_call_target="tpu_custom_call" | custom-call | tf_op jit(solution)/shard_map/pallas_call | solution.py:252
  30.3 0.0 copy-start.2
  30.3 0.7 %copy-done.2 = f32[6,64]{1,0:T(8,128)S(1)} copy-done((f32[6,64]{1,0:T(8,128)S(1)}, f32[6,64]{1,0:T(8,128)}, u32[]{:S(2)}) %copy-start.2) | copy-done | bytes 1560
  31.0 0.0 copy-start.1
  31.0 0.6 %copy.14 = f32[6,64]{1,0:T(8,128)} copy(f32[6,64]{1,0:T(8,128)S(1)} %copy-done.2) | data formatting | bytes 3072
  31.6 0.1 copy-done.1
  31.7 0.0 copy-start
  31.7 0.6 %copy.15 = f32[8,128]{1,0:T(8,128)} copy(f32[8,128]{1,0:T(8,128)S(1)} %copy-done.1) | data formatting | bytes 8192
  32.3 0.1 copy-done
  32.3 0.6 %copy.16 = f32[8,128]{1,0:T(8,128)} copy(f32[8,128]{1,0:T(8,128)S(1)} %copy-done) | data formatting | bytes 8192
Async XLA Ops:
  30.3 0.7 %copy-start.2 = (f32[6,64]{1,0:T(8,128)S(1)}, f32[6,64]{1,0:T(8,128)}, u32[]{:S(2)}) copy-start(f32[6,64]{1,0:T(8,128)} %get-tuple-element.6) | copy-start | bytes 4612
  31.0 0.7 %copy-start.1 = (f32[8,128]{1,0:T(8,128)S(1)}, f32[8,128]{1,0:T(8,128)}, u32[]{:S(2)}) copy-start(f32[8,128]{1,0:T(8,128)} %get-tuple-element.7) | copy-start | bytes 12292
  31.7 0.7 %copy-start = (f32[8,128]{1,0:T(8,128)S(1)}, f32[8,128]{1,0:T(8,128)}, u32[]{:S(2)}) copy-start(f32[8,128]{1,0:T(8,128)} %get-tuple-element.8) | copy-start | bytes 12292

commit v2 on v1

--- a/solution.py
+++ b/solution.py
@@ -47,34 +47,48 @@
 
 def inverse_spd(gram):
     size = gram.shape[0]
+    wide = 2 * size
     eye = (iota((size, size), 0) == iota((size, size), 1)).astype(F32)
-    wide = jnp.concatenate([eye, gram], axis=1)
-    blocks = [wide[ROWS * b : ROWS * (b + 1), :] for b in range(size // ROWS)]
-    below = iota((ROWS, 1), 0)
-    for k in range(size):
-        first, r = k // ROWS, k % ROWS
-        row = blocks[first][r : r + 1, :]
-        scaled = row * (1.0 / row[:, size + k : size + k + 1])
-        for b in range(first, len(blocks)):
-            if b == first and r == ROWS - 1:
-                continue
-            column = blocks[b][:, size + k : size + k + 1]
-            if b == first:
-                column = jnp.where(below > r, column, 0.0)
-            blocks[b] = blocks[b] - column * scaled
-    done = jnp.concatenate(blocks, axis=0)
-    on_diag = iota(done.shape, 0) + size == iota(done.shape, 1)
-    pivots = jnp.sum(jnp.where(on_diag, done, 0.0), axis=1, keepdims=True)
-    lower = done[:, :size]
-    return dot_tn(lower, lower / pivots)
+    joined = jnp.concatenate([eye, gram], axis=1)
+    blocks = [joined[ROWS * b : ROWS * (b + 1), :] for b in range(size // ROWS)]
+    row_of = iota((ROWS, wide), 0)
+    for p in range(size // ROWS):
+        spread = [
+            [
+                jnp.broadcast_to(block[:, size + p * ROWS + c : size + p * ROWS + c + 1], (ROWS, wide))
+                for c in range(ROWS)
+            ]
+            for block in blocks
+        ]
+        panel = blocks[p]
+        columns = list(spread[p])
+        for k in range(ROWS):
+            pivot = columns[k]
+            scale = 1.0 / pivot[k : k + 1, :]
+            here = row_of == k
+            top = panel[k : k + 1, :] * scale
+            panel = jnp.where(here, top, panel - pivot * top)
+            for c in range(k + 1, ROWS):
+                top = columns[c][k : k + 1, :] * scale
+                columns[c] = jnp.where(here, top, columns[c] - pivot * top)
+        for b in range(len(blocks)):
+            if b == p:
+                blocks[b] = panel
+            else:
+                terms = [spread[b][c] * panel[c : c + 1, :] for c in range(ROWS)]
+                while len(terms) > 1:
+                    terms = [x + y for x, y in zip(terms[::2], terms[1::2])]
+                blocks[b] = blocks[b] - terms[0]
+    return jnp.concatenate(blocks, axis=0)[:, :size]
 
 
 def kernel(
     wafers, spans,
-    ts_ref, tm_ref, bg_ref, dw_ref, cs_ref, cl_ref, pt_ref, ht_ref,
+    ts_ref, tm_hbm, bg_hbm, dw_hbm, cs_hbm, cl_hbm, pt_hbm, ht_hbm,
     fit_ref, rhs_ref, wgt_ref,
+    tm_ref, bg_ref, dw_ref, cs_ref, cl_ref, pt_ref, ht_ref,
     ts_rx, ts_all, gr_rx, pj_rx, sw_ref, val_ref, hot_ref, tx, rx,
-    span_send, span_recv, tile_send, tile_recv,
+    span_send, span_recv, tile_send, tile_recv, local_sem,
 ):
     det_dev = ts_ref.shape[0]
     nt, span_len = tm_ref.shape
@@ -85,22 +99,43 @@
     my_w, my_s = lax.axis_index("wafer"), lax.axis_index("span")
     me = my_w * spans + my_s
 
-    def peer(i):
-        other = lax.rem(me + i, total)
-        return other, lax.div(other, spans), lax.rem(other, spans)
-
+    s_peers = [lax.rem(my_s + i, spans) for i in range(spans)]
+    w_peers = [lax.rem(my_w + i, wafers) for i in range(wafers)]
+    others = s_peers[1:]
+
+    def for_peers(act):
+        if total <= 64:
+            for s in range(spans):
+                for w in range(wafers):
+                    if w or s:
+                        act(w_peers[w], s_peers[s])
+        else:
+
+            def step(i, carry):
+                other = lax.rem(me + i, total)
+                act(lax.div(other, spans), lax.rem(other, spans))
+                return carry
+
+            lax.fori_loop(1, total, step, 0)
+
+    def own_start(s):
+        return pl.multiple_of(s * span_len, span_len)
+
+    pairs = (
+        (tm_hbm, tm_ref),
+        (ts_ref.at[:, pl.ds(own_start(my_s), span_len)], ts_rx.at[my_s]),
+        (pt_hbm, pt_ref), (cs_hbm, cs_ref), (cl_hbm, cl_ref), (dw_hbm, dw_ref), (ht_hbm, ht_ref), (bg_hbm, bg_ref),
+    )
+    local = [pltpu.make_async_copy(a, b, local_sem.at[i]) for i, (a, b) in enumerate(pairs)]
+    for copy in local:
+        copy.start()
     barrier = pltpu.get_barrier_semaphore()
-
-    def greet(i, carry):
-        unused, w, s = peer(i)
-        pl.semaphore_signal(barrier, inc=1, device_id=(w, s), device_id_type=MESH)
-        return carry
-
-    lax.fori_loop(1, total, greet, 0)
-
+    for_peers(
+        lambda w, s: pl.semaphore_signal(barrier, inc=1, device_id=(w, s), device_id_type=MESH)
+    )
+    local[0].wait()
     templates = tm_ref[...]
     gr_rx[my_s] = dot_nt(templates, templates)
-    ts_rx[my_s] = ts_ref[:, pl.ds(pl.multiple_of(my_s * span_len, span_len), span_len)]
     pl.semaphore_wait(barrier, total - 1)
 
     def to_span(src, dst, which, s):
@@ -113,12 +148,13 @@
         slots = buffer.at[pl.ds(0, spans - 1)]
         pltpu.make_async_copy(slots, slots, sems.at[which]).wait()
 
-    others = [lax.rem(my_s + i, spans) for i in range(1, spans)]
     for s in others:
-        start = pl.multiple_of(s * span_len, span_len)
-        to_span(ts_ref.at[:, pl.ds(start, span_len)], ts_rx.at[my_s], 0, s)
+        to_span(ts_ref.at[:, pl.ds(own_start(s), span_len)], ts_rx.at[my_s], 0, s)
     for s in others:
         to_span(gr_rx.at[my_s], gr_rx.at[my_s], 1, s)
+
+    for copy in local[2:]:
+        copy.wait()
 
     listed = ht_ref[...]
     owner = lax.shift_right_logical(listed, jnp.full(listed.shape, log2(TILE_OWN), jnp.int32)).astype(F32)
@@ -159,19 +195,29 @@
             coarse = coarse_of(points)
             fine = points & (pix - 1)
             values = source[rows, :]
-            for r in range(ROWS):
-                left = jnp.where(coarse_iota == coarse[r : r + 1, :], values[r : r + 1, :], 0.0).astype(BF16)
-                if first_time:
-                    right = jnp.where(fine_iota == fine[r : r + 1, :], 1.0, 0.0).astype(BF16)
-                    hot_ref[g * ROWS + r] = right
-                else:
-                    right = hot_ref[g * ROWS + r]
-                acc = acc + lax.dot_general(
-                    left, right, (((1,), (1,)), ((), ())), preferred_element_type=F32
+            left = jnp.concatenate(
+                [
+                    jnp.where(coarse_iota == coarse[r : r + 1, :], values[r : r + 1, :], 0.0).astype(BF16)
+                    for r in range(ROWS)
+                ],
+                axis=1,
+            )
+            if first_time:
+                right = jnp.concatenate(
+                    [
+                        jnp.where(fine_iota == fine[r : r + 1, :], 1.0, 0.0).astype(BF16)
+                        for r in range(ROWS)
+                    ],
+                    axis=1,
                 )
-            return acc
-
-        return lax.fori_loop(0, det_w // ROWS, step, jnp.zeros((coarse_count, pix), F32))
+                hot_ref[g] = right
+            else:
+                right = hot_ref[g]
+            return acc + lax.dot_general(
+                left, right, (((1,), (1,)), ((), ())), preferred_element_type=F32
+            )
+
+        return lax.fori_loop(0, det_w // ROWS, step, jnp.zeros((coarse_count, pix), F32), unroll=2)
 
     def send_tiles(part, m):
         wide = jnp.concatenate([part[q * hits : (q + 1) * hits, :] for q in range(wafers)], axis=1)
@@ -181,16 +227,14 @@
                 tx[m, q * spans + o] = out[o * CAP : (o + 1) * CAP, q * pix : (q + 1) * pix]
         rx[m, me] = tx[m, me]
 
-        def send(i, carry):
-            other, w, s = peer(i)
+        def send(w, s):
             pltpu.make_async_remote_copy(
-                src_ref=tx.at[m, other], dst_ref=rx.at[m, me],
+                src_ref=tx.at[m, w * spans + s], dst_ref=rx.at[m, me],
                 send_sem=tile_send.at[m], recv_sem=tile_recv.at[m],
                 device_id=(w, s), device_id_type=MESH,
             ).start()
-            return carry
-
-        lax.fori_loop(1, total, send, 0)
+
+        for_peers(send)
 
     def tile_wait(buffer, sems, m):
         part = buffer.at[m, pl.ds(0, total - 1)]
@@ -210,6 +254,7 @@
     send_tiles(bin_rows(sw_ref, True), 1)
 
     same_line = (bg_ref[...].astype(F32) == to_column(bg_ref[...])).astype(F32)
+    local[1].wait()
     span_wait(ts_rx, span_recv, 0)
     for s in range(spans):
         ts_all[s * det_dev : (s + 1) * det_dev, :] = ts_rx[s]
@@ -241,6 +286,15 @@
         tile_wait(tx, tile_send, m)
 
 
+def hand_on(*refs):
+    sems = refs[6]
+    copies = [pltpu.make_async_copy(refs[i], refs[3 + i], sems.at[i]) for i in range(3)]
+    for copy in copies:
+        copy.start()
+    for copy in copies:
+        copy.wait()
+
+
 def body(timestream, templates, bias_group, det_weight, cut_start, cut_len, pointing, hit_tiles):
     wafers, spans = lax.axis_size("wafer"), lax.axis_size("span")
     det_dev = timestream.shape[0]
@@ -249,29 +303,38 @@
     pix = TILE // wafers
     total = wafers * spans
     vmem = pl.BlockSpec(memory_space=pltpu.VMEM)
-    return pl.pallas_call(
+    results = (
+        jax.ShapeDtypeStruct((det_dev, nt), F32),
+        jax.ShapeDtypeStruct((TILE_OWN, pix), F32),
+        jax.ShapeDtypeStruct((TILE_OWN, pix), F32),
+    )
+    outs = pl.pallas_call(
         functools.partial(kernel, wafers, spans),
-        out_shape=(
-            jax.ShapeDtypeStruct((det_dev, nt), F32),
-            jax.ShapeDtypeStruct((TILE_OWN, pix), F32),
-            jax.ShapeDtypeStruct((TILE_OWN, pix), F32),
-        ),
-        in_specs=[vmem] * 8,
+        out_shape=results,
+        in_specs=[pl.BlockSpec(memory_space=pl.ANY)] * 8,
         out_specs=(vmem,) * 3,
         scratch_shapes=[
+            pltpu.VMEM((nt, span_len), F32),
+            pltpu.VMEM((1, det_w), jnp.int32),
+            pltpu.VMEM((1, det_w), F32),
+            pltpu.VMEM((1, det_w), jnp.int32),
+            pltpu.VMEM((1, det_w), jnp.int32),
+            pltpu.VMEM((det_w, span_len), jnp.int32),
+            pltpu.VMEM(hit_tiles.shape, jnp.int32),
             pltpu.VMEM((spans, det_dev, span_len), F32),
             pltpu.VMEM((det_w, span_len), F32),
             pltpu.VMEM((spans, nt, nt), F32),
             pltpu.VMEM((spans, det_w, nt), F32),
             pltpu.VMEM((det_w, span_len), F32),
             pltpu.VMEM((det_w, span_len), F32),
-            pltpu.VMEM((det_w, pix, span_len), BF16),
+            pltpu.VMEM((det_w // ROWS, pix, ROWS * span_len), BF16),
             pltpu.VMEM((2, total, CAP, pix), F32),
             pltpu.VMEM((2, total, CAP, pix), F32),
             pltpu.SemaphoreType.DMA((3,)),
             pltpu.SemaphoreType.DMA((3,)),
             pltpu.SemaphoreType.DMA((2,)),
             pltpu.SemaphoreType.DMA((2,)),
+            pltpu.SemaphoreType.DMA((8,)),
         ],
         compiler_params=pltpu.CompilerParams(
             collective_id=0, has_side_effects=True, vmem_limit_bytes=56 * 1024 * 1024
@@ -280,6 +343,14 @@
         timestream, templates, bias_group.reshape(1, det_w), det_weight.reshape(1, det_w),
         cut_start.reshape(1, det_w), cut_len.reshape(1, det_w), pointing, hit_tiles,
     )
+    anywhere = pl.BlockSpec(memory_space=pl.ANY)
+    return pl.pallas_call(
+        hand_on,
+        out_shape=results,
+        in_specs=[anywhere] * 3,
+        out_specs=(anywhere,) * 3,
+        scratch_shapes=[pltpu.SemaphoreType.DMA((3,))],
+    )(*outs)
 
 
 def solution(mesh):

time: 33.2 us -> 29.5 us (0.89)
  local copies, waits for them, and re-layouts: 2.62 us -> 0 us
  Pallas kernels: 29.7 us -> 28.7 us
    unnamed x9 -> x0, local copies, waits for them, and re-layouts: 2.62 us -> none
    pallas_call x1 -> x2, Pallas kernels: 29.7 us -> 28.7 us  [the longest x1 27.2 us: body(): pl.pallas_call(functools.partial(kernel, wafers, spans), out_shape=result...]
where the time goes in v2:
time: 29.5 us; the launch traced here: 29.3 us
  Pallas kernels  28.7 us (97%)
  between operations  0.64 us (2%)
    pallas_call x1, Pallas kernels, body(): pl.pallas_call(functools.partial(kernel, wafers, spans), out_shape=result...  27.2 us
    pallas_call x1, Pallas kernels, body(): pl.pallas_call(hand_on, out_shape=results, in_specs=[anywhere] * 3, out_s...  1.47 us

profile of v2, /device:TPU:0, one launch (start us, length us, event | category | flops | bytes accessed | tf_op | source)
XLA Modules:
  0.0 29.3 jit_solution(1400676031914660951)
XLA Ops:
  0.6 27.2 %shard_map.103 = (f32[6,64]{1,0:T(8,128)}, f32[8,128]{1,0:T(8,128)}, f32[8,128]{1,0:T(8,128)}) custom-call(f32[6,2048]{1,0:T(8,128)} %ts_ref.1, f32[64,256]{1,0:T(8,128)} %tm_hbm.1, s32[1,48]{1,0:T(1,128)} %bitcast.4, f32[1,48]{1,0:T(1,128)} %bitcast.5, s32[1,48]{1,0:T(1,128)} %bitcast.6, s32[1,48]{1,0:T(1,128)} %bitcast.7, s32[48,256]{1,0:T(8,128)} %pt_hbm.1, ...), custom_call_target="tpu_custom_call" | custom-call | tf_op jit(solution)/shard_map/pallas_call | solution.py:311
  27.8 1.5 %shard_map.104 = (f32[6,64]{1,0:T(8,128)}, f32[8,128]{1,0:T(8,128)}, f32[8,128]{1,0:T(8,128)}) custom-call(f32[6,64]{1,0:T(8,128)} %get-tuple-element.6.refs_0_, f32[8,128]{1,0:T(8,128)} %get-tuple-element.7.refs_1_, f32[8,128]{1,0:T(8,128)} %get-tuple-element.8.refs_2_), custom_call_target="tpu_custom_call" | custom-call | tf_op jit(solution)/shard_map/pallas_call | solution.py:347

commit v3 on v2

--- a/solution.py
+++ b/solution.py
@@ -32,6 +32,15 @@
 
 def iota(shape, dim):
     return lax.broadcasted_iota(jnp.int32, shape, dim)
+
+
+def dot_selected(selector, values):
+    high = values.astype(BF16)
+    rest = values - high.astype(F32)
+    middle = rest.astype(BF16)
+    low = (rest - middle.astype(F32)).astype(BF16)
+    out = [jnp.dot(selector, part, preferred_element_type=F32) for part in (low, middle, high)]
+    return (out[0] + out[1]) + out[2]
 
 
 def to_column(row):
@@ -82,12 +91,21 @@
     return jnp.concatenate(blocks, axis=0)[:, :size]
 
 
+def slot_codes(listed):
+    owner = lax.shift_right_logical(listed, jnp.full(listed.shape, log2(TILE_OWN), jnp.int32)).astype(F32)
+    lane = iota(listed.shape, 1)
+    rank = jnp.zeros(listed.shape, F32)
+    for j in range(listed.shape[1] - 1):
+        rank += jnp.where((owner[:, j : j + 1] == owner) & (lane > j), 1.0, 0.0)
+    return owner * CAP + rank
+
+
 def kernel(
     wafers, spans,
     ts_ref, tm_hbm, bg_hbm, dw_hbm, cs_hbm, cl_hbm, pt_hbm, ht_hbm,
-    fit_ref, rhs_ref, wgt_ref,
+    fit_hbm, rx,
     tm_ref, bg_ref, dw_ref, cs_ref, cl_ref, pt_ref, ht_ref,
-    ts_rx, ts_all, gr_rx, pj_rx, sw_ref, val_ref, hot_ref, tx, rx,
+    ts_rx, ts_all, gr_rx, pj_rx, sw_ref, val_ref, hot_ref, left_ref, tx, fit_ref,
     span_send, span_recv, tile_send, tile_recv, local_sem,
 ):
     det_dev = ts_ref.shape[0]
@@ -127,15 +145,12 @@
         (pt_hbm, pt_ref), (cs_hbm, cs_ref), (cl_hbm, cl_ref), (dw_hbm, dw_ref), (ht_hbm, ht_ref), (bg_hbm, bg_ref),
     )
     local = [pltpu.make_async_copy(a, b, local_sem.at[i]) for i, (a, b) in enumerate(pairs)]
-    for copy in local:
-        copy.start()
     barrier = pltpu.get_barrier_semaphore()
     for_peers(
         lambda w, s: pl.semaphore_signal(barrier, inc=1, device_id=(w, s), device_id_type=MESH)
     )
-    local[0].wait()
-    templates = tm_ref[...]
-    gr_rx[my_s] = dot_nt(templates, templates)
+    for copy in local:
+        copy.start()
     pl.semaphore_wait(barrier, total - 1)
 
     def to_span(src, dst, which, s):
@@ -150,27 +165,19 @@
 
     for s in others:
         to_span(ts_ref.at[:, pl.ds(own_start(s), span_len)], ts_rx.at[my_s], 0, s)
+    local[0].wait()
+    templates = tm_ref[...]
+    gr_rx[my_s] = dot_nt(templates, templates)
     for s in others:
         to_span(gr_rx.at[my_s], gr_rx.at[my_s], 1, s)
 
     for copy in local[2:]:
         copy.wait()
 
-    listed = ht_ref[...]
-    owner = lax.shift_right_logical(listed, jnp.full(listed.shape, log2(TILE_OWN), jnp.int32)).astype(F32)
-    lane = iota(listed.shape, 1)
-    rank = jnp.zeros(listed.shape, F32)
-    for j in range(hits - 1):
-        rank += jnp.where((owner[:, j : j + 1] == owner) & (lane > j), 1.0, 0.0)
-    code = owner * CAP + rank
-    own_code = jnp.sum(jnp.where(iota(listed.shape, 0) == my_s, code, 0.0), axis=0, keepdims=True)
+    code = slot_codes(ht_ref[...])
+    own_code = jnp.sum(jnp.where(iota(code.shape, 0) == my_s, code, 0.0), axis=0, keepdims=True)
     slots = spans * CAP
-    selector = (own_code == iota((slots, hits), 0).astype(F32)).astype(F32)
-    landing = []
-    for k in range(CAP):
-        mine = code == (my_s * CAP + k).astype(F32)
-        place = (listed - (my_s * TILE_OWN - 1)).astype(F32)
-        landing.append(jnp.sum(jnp.where(mine, place, 0.0), axis=1, keepdims=True) - 1.0)
+    selector = (own_code == iota((slots, hits), 0).astype(F32)).astype(BF16)
 
     time = (iota((det_w, span_len), 1) + my_s * span_len).astype(F32)
     cut_start = to_column(cs_ref[...])
@@ -188,70 +195,33 @@
     def coarse_of(points):
         return (shifted(points, log2(pix)) & (wafers - 1)) * hits + shifted(points, log2(TILE))
 
-    def bin_rows(source, first_time):
-        def step(g, acc):
-            rows = pl.ds(pl.multiple_of(g * ROWS, ROWS), ROWS)
-            points = pt_ref[rows, :]
-            coarse = coarse_of(points)
-            fine = points & (pix - 1)
-            values = source[rows, :]
-            left = jnp.concatenate(
-                [
-                    jnp.where(coarse_iota == coarse[r : r + 1, :], values[r : r + 1, :], 0.0).astype(BF16)
-                    for r in range(ROWS)
-                ],
-                axis=1,
-            )
-            if first_time:
-                right = jnp.concatenate(
-                    [
-                        jnp.where(fine_iota == fine[r : r + 1, :], 1.0, 0.0).astype(BF16)
-                        for r in range(ROWS)
-                    ],
-                    axis=1,
-                )
-                hot_ref[g] = right
-            else:
-                right = hot_ref[g]
-            return acc + lax.dot_general(
-                left, right, (((1,), (1,)), ((), ())), preferred_element_type=F32
-            )
-
-        return lax.fori_loop(0, det_w // ROWS, step, jnp.zeros((coarse_count, pix), F32), unroll=2)
-
-    def send_tiles(part, m):
-        wide = jnp.concatenate([part[q * hits : (q + 1) * hits, :] for q in range(wafers)], axis=1)
-        out = dot_nn(selector, wide)
-        for q in range(wafers):
-            for o in range(spans):
-                tx[m, q * spans + o] = out[o * CAP : (o + 1) * CAP, q * pix : (q + 1) * pix]
-        rx[m, me] = tx[m, me]
-
-        def send(w, s):
-            pltpu.make_async_remote_copy(
-                src_ref=tx.at[m, w * spans + s], dst_ref=rx.at[m, me],
-                send_sem=tile_send.at[m], recv_sem=tile_recv.at[m],
-                device_id=(w, s), device_id_type=MESH,
-            ).start()
-
-        for_peers(send)
-
-    def tile_wait(buffer, sems, m):
-        part = buffer.at[m, pl.ds(0, total - 1)]
-        pltpu.make_async_copy(part, part, sems.at[m]).wait()
-
-    def collect(m):
-        row_iota = iota((TILE_OWN, pix), 0).astype(F32)
-        acc = jnp.zeros((TILE_OWN, pix), F32)
-        for s in range(spans):
-            arrived = rx[m, s]
-            for w in range(1, wafers):
-                arrived = arrived + rx[m, w * spans + s]
-            for k in range(CAP):
-                acc = acc + jnp.where(row_iota == landing[k][s : s + 1, :], arrived[k : k + 1, :], 0.0)
-        return acc
-
-    send_tiles(bin_rows(sw_ref, True), 1)
+    groups = det_w // ROWS
+    keep_left = left_ref.shape[0] == groups
+
+    def place(coarse, values):
+        return jnp.concatenate(
+            [
+                jnp.where(coarse_iota == coarse[r : r + 1, :], values[r : r + 1, :], 0.0).astype(BF16)
+                for r in range(ROWS)
+            ],
+            axis=1,
+        )
+
+    def rows_of(g):
+        return pl.ds(g * ROWS if isinstance(g, int) else pl.multiple_of(g * ROWS, ROWS), ROWS)
+
+    def prepare(g, carry):
+        points = pt_ref[rows_of(g), :]
+        fine = points & (pix - 1)
+        hot_ref[g] = jnp.concatenate(
+            [jnp.where(fine_iota == fine[r : r + 1, :], 1.0, 0.0).astype(BF16) for r in range(ROWS)],
+            axis=1,
+        )
+        if keep_left:
+            left_ref[g] = place(coarse_of(points), sw_ref[rows_of(g), :])
+        return carry
+
+    lax.fori_loop(0, groups, prepare, 0, unroll=2)
 
     same_line = (bg_ref[...].astype(F32) == to_column(bg_ref[...])).astype(F32)
     local[1].wait()
@@ -272,27 +242,90 @@
     projection = jnp.sum(pj_rx[...], axis=0)
     filtered = cleaned - dot_nn(projection, solved)
     val_ref[...] = (sw_ref[...] * filtered).astype(BF16).astype(F32)
-    send_tiles(bin_rows(val_ref, False), 0)
+
+    def bin_group(g, part):
+        coarse = coarse_of(pt_ref[rows_of(g), :])
+        weights = left_ref[g] if keep_left else place(coarse, sw_ref[rows_of(g), :])
+        left = jnp.concatenate([place(coarse, val_ref[rows_of(g), :]), weights], axis=0)
+        return part + lax.dot_general(
+            left, hot_ref[g], (((1,), (1,)), ((), ())), preferred_element_type=F32
+        )
+
+    part = jnp.zeros((2 * coarse_count, pix), F32)
+    if groups <= 8:
+        for g in range(groups):
+            part = bin_group(g, part)
+    else:
+        part = lax.fori_loop(0, groups, bin_group, part)
+
+    wide = jnp.concatenate([part[q * hits : (q + 1) * hits, :] for q in range(2 * wafers)], axis=1)
+    out = dot_selected(selector, wide)
+    for q in range(wafers):
+        for o in range(spans):
+            for m in range(2):
+                start = (m * wafers + q) * pix
+                tx[q * spans + o, m * CAP : (m + 1) * CAP] = out[
+                    o * CAP : (o + 1) * CAP, start : start + pix
+                ]
+
+    def send(w, s):
+        pltpu.make_async_remote_copy(
+            src_ref=tx.at[w * spans + s], dst_ref=rx.at[me],
+            send_sem=tile_send, recv_sem=tile_recv,
+            device_id=(w, s), device_id_type=MESH,
+        ).start()
+
+    for_peers(send)
+    own = pltpu.make_async_copy(tx.at[me], rx.at[me], local_sem.at[0])
+    own.start()
 
     mine = (iota((det_dev, det_w), 1) == iota((det_dev, det_w), 0) + my_s * det_dev).astype(F32)
     fit_ref[...] = dot_nn(dot_nn(mine, projection), inverse)
-    tile_wait(rx, tile_recv, 1)
-    wgt_ref[...] = collect(1)
-    tile_wait(rx, tile_recv, 0)
-    rhs_ref[...] = collect(0)
+    fit = pltpu.make_async_copy(fit_ref, fit_hbm, local_sem.at[1])
+    fit.start()
     for which, buffer in enumerate((ts_rx, gr_rx, pj_rx)):
         span_wait(buffer, span_send, which)
-    for m in range(2):
-        tile_wait(tx, tile_send, m)
-
-
-def hand_on(*refs):
-    sems = refs[6]
-    copies = [pltpu.make_async_copy(refs[i], refs[3 + i], sems.at[i]) for i in range(3)]
-    for copy in copies:
-        copy.start()
-    for copy in copies:
-        copy.wait()
+    own.wait()
+    fit.wait()
+    arrivals, departures = rx.at[pl.ds(0, total - 1)], tx.at[pl.ds(0, total - 1)]
+    pltpu.make_async_copy(departures, departures, tile_send).wait()
+    pltpu.make_async_copy(arrivals, arrivals, tile_recv).wait()
+
+
+def collect(
+    wafers, spans, rx_hbm, fit_hbm, ht_hbm, fit_out, rhs_ref, wgt_ref, rx, ht_ref, sems
+):
+    arrivals = pltpu.make_async_copy(rx_hbm, rx, sems.at[0])
+    listing = pltpu.make_async_copy(ht_hbm, ht_ref, sems.at[1])
+    fit = pltpu.make_async_copy(fit_hbm, fit_out, sems.at[2])
+    listing.start()
+    arrivals.start()
+    fit.start()
+    my_s = lax.axis_index("span")
+    pix = rhs_ref.shape[1]
+    listing.wait()
+    listed = ht_ref[...]
+    code = slot_codes(listed)
+    place = (listed - (my_s * TILE_OWN - 1)).astype(F32)
+    landing = [
+        jnp.sum(jnp.where(code == (my_s * CAP + k).astype(F32), place, 0.0), axis=1, keepdims=True) - 1.0
+        for k in range(CAP)
+    ]
+    row_iota = iota((TILE_OWN, pix), 0).astype(F32)
+    sums = [jnp.zeros((TILE_OWN, pix), F32) for m in range(2)]
+    arrivals.wait()
+    for s in range(spans):
+        arrived = rx[s]
+        for w in range(1, wafers):
+            arrived = arrived + rx[w * spans + s]
+        for k in range(CAP):
+            here = row_iota == landing[k][s : s + 1, :]
+            for m in range(2):
+                row = m * CAP + k
+                sums[m] = sums[m] + jnp.where(here, arrived[row : row + 1, :], 0.0)
+    rhs_ref[...] = sums[0]
+    wgt_ref[...] = sums[1]
+    fit.wait()
 
 
 def body(timestream, templates, bias_group, det_weight, cut_start, cut_len, pointing, hit_tiles):
@@ -303,16 +336,16 @@
     pix = TILE // wafers
     total = wafers * spans
     vmem = pl.BlockSpec(memory_space=pltpu.VMEM)
-    results = (
-        jax.ShapeDtypeStruct((det_dev, nt), F32),
-        jax.ShapeDtypeStruct((TILE_OWN, pix), F32),
-        jax.ShapeDtypeStruct((TILE_OWN, pix), F32),
-    )
-    outs = pl.pallas_call(
+    anywhere = pl.BlockSpec(memory_space=pl.ANY)
+    fit_shape = jax.ShapeDtypeStruct((det_dev, nt), F32)
+    map_shape = jax.ShapeDtypeStruct((TILE_OWN, pix), F32)
+    hits = hit_tiles.shape[1]
+    groups = det_w // ROWS
+    fit, tiles = pl.pallas_call(
         functools.partial(kernel, wafers, spans),
-        out_shape=results,
-        in_specs=[pl.BlockSpec(memory_space=pl.ANY)] * 8,
-        out_specs=(vmem,) * 3,
+        out_shape=(fit_shape, jax.ShapeDtypeStruct((total, 2 * CAP, pix), F32)),
+        in_specs=[anywhere] * 8,
+        out_specs=(anywhere,) * 2,
         scratch_shapes=[
             pltpu.VMEM((nt, span_len), F32),
             pltpu.VMEM((1, det_w), jnp.int32),
@@ -327,13 +360,14 @@
             pltpu.VMEM((spans, det_w, nt), F32),
             pltpu.VMEM((det_w, span_len), F32),
             pltpu.VMEM((det_w, span_len), F32),
-            pltpu.VMEM((det_w // ROWS, pix, ROWS * span_len), BF16),
-            pltpu.VMEM((2, total, CAP, pix), F32),
-            pltpu.VMEM((2, total, CAP, pix), F32),
+            pltpu.VMEM((groups, pix, ROWS * span_len), BF16),
+            pltpu.VMEM((groups if groups <= 8 else 1, wafers * hits, ROWS * span_len), BF16),
+            pltpu.VMEM((total, 2 * CAP, pix), F32),
+            pltpu.VMEM((det_dev, nt), F32),
             pltpu.SemaphoreType.DMA((3,)),
             pltpu.SemaphoreType.DMA((3,)),
-            pltpu.SemaphoreType.DMA((2,)),
-            pltpu.SemaphoreType.DMA((2,)),
+            pltpu.SemaphoreType.DMA,
+            pltpu.SemaphoreType.DMA,
             pltpu.SemaphoreType.DMA((8,)),
         ],
         compiler_params=pltpu.CompilerParams(
@@ -343,14 +377,17 @@
         timestream, templates, bias_group.reshape(1, det_w), det_weight.reshape(1, det_w),
         cut_start.reshape(1, det_w), cut_len.reshape(1, det_w), pointing, hit_tiles,
     )
-    anywhere = pl.BlockSpec(memory_space=pl.ANY)
     return pl.pallas_call(
-        hand_on,
-        out_shape=results,
+        functools.partial(collect, wafers, spans),
+        out_shape=(fit_shape, map_shape, map_shape),
         in_specs=[anywhere] * 3,
-        out_specs=(anywhere,) * 3,
-        scratch_shapes=[pltpu.SemaphoreType.DMA((3,))],
-    )(*outs)
+        out_specs=(anywhere, vmem, vmem),
+        scratch_shapes=[
+            pltpu.VMEM((total, 2 * CAP, pix), F32),
+            pltpu.VMEM(hit_tiles.shape, jnp.int32),
+            pltpu.SemaphoreType.DMA((3,)),
+        ],
+    )(tiles, fit, hit_tiles)
 
 
 def solution(mesh):

time: 29.5 us -> 28.4 us (0.963)
  Pallas kernels: 28.7 us -> 27.6 us
    pallas_call x2, Pallas kernels: 28.7 us -> 27.6 us  [the longest x1 25.8 us: body(): pl.pallas_call(functools.partial(kernel, wafers, spans), out_shape=(fit_s...]
where the time goes in v3:
time: 28.4 us; the launch traced here: 28.2 us
  Pallas kernels  27.6 us (97%)
  between operations  0.64 us (2%)
    pallas_call x1, Pallas kernels, body(): pl.pallas_call(functools.partial(kernel, wafers, spans), out_shape=(fit_s...  25.8 us
    pallas_call x1, Pallas kernels, body(): pl.pallas_call(functools.partial(collect, wafers, spans), out_shape=(fit_...  1.82 us

profile of v3, /device:TPU:0, one launch (start us, length us, event | category | flops | bytes accessed | tf_op | source)
XLA Modules:
  0.0 28.2 jit_solution(17889804835502958149)
XLA Ops:
  0.6 25.8 %shard_map.103 = (f32[6,64]{1,0:T(8,128)}, f32[32,4,128]{2,1,0:T(4,128)}) custom-call(f32[6,2048]{1,0:T(8,128)} %ts_ref.1, f32[64,256]{1,0:T(8,128)} %tm_hbm.1, s32[1,48]{1,0:T(1,128)} %bitcast.4, f32[1,48]{1,0:T(1,128)} %bitcast.5, s32[1,48]{1,0:T(1,128)} %bitcast.6, s32[1,48]{1,0:T(1,128)} %bitcast.7, s32[48,256]{1,0:T(8,128)} %pt_hbm.1, s32[8,8]{1,0:T(8,128)} %ht_hbm.3), custom_call_target="tpu_custom_call" | custom-call | tf_op jit(solution)/shard_map/pallas_call | solution.py:344
  26.4 1.8 %shard_map.104 = (f32[6,64]{1,0:T(8,128)}, f32[8,128]{1,0:T(8,128)}, f32[8,128]{1,0:T(8,128)}) custom-call(f32[32,4,128]{2,1,0:T(4,128)} %get-tuple-element.5.rx_hbm, f32[6,64]{1,0:T(8,128)} %get-tuple-element.6.fit_hbm, s32[8,8]{1,0:T(8,128)} %ht_hbm.3), custom_call_target="tpu_custom_call" | custom-call | tf_op jit(solution)/shard_map/pallas_call | solution.py:380

commit v4 on v3

--- a/solution.py
+++ b/solution.py
@@ -91,6 +91,16 @@
     return jnp.concatenate(blocks, axis=0)[:, :size]
 
 
+def pack(tall):
+    half = tall.shape[0] // 2
+    return jnp.concatenate([tall[:half, :], tall[half:, :]], axis=1)
+
+
+def unpack(wide):
+    half = wide.shape[1] // 2
+    return jnp.concatenate([wide[:, :half], wide[:, half:]], axis=0)
+
+
 def slot_codes(listed):
     owner = lax.shift_right_logical(listed, jnp.full(listed.shape, log2(TILE_OWN), jnp.int32)).astype(F32)
     lane = iota(listed.shape, 1)
@@ -105,36 +115,18 @@
     ts_ref, tm_hbm, bg_hbm, dw_hbm, cs_hbm, cl_hbm, pt_hbm, ht_hbm,
     fit_hbm, rx,
     tm_ref, bg_ref, dw_ref, cs_ref, cl_ref, pt_ref, ht_ref,
-    ts_rx, ts_all, gr_rx, pj_rx, sw_ref, val_ref, hot_ref, left_ref, tx, fit_ref,
-    span_send, span_recv, tile_send, tile_recv, local_sem,
+    ts_rx, ts_all, gr_rx, pj_rx, sw_ref, val_ref, hot_ref, left_ref, wafer_tx, wafer_rx, tx, fit_ref,
+    span_send, span_recv, wafer_send, wafer_recv, local_sem,
 ):
     det_dev = ts_ref.shape[0]
     nt, span_len = tm_ref.shape
     det_w = pt_ref.shape[0]
     hits = ht_ref.shape[1]
-    total = wafers * spans
     pix = TILE // wafers
     my_w, my_s = lax.axis_index("wafer"), lax.axis_index("span")
-    me = my_w * spans + my_s
-
-    s_peers = [lax.rem(my_s + i, spans) for i in range(spans)]
-    w_peers = [lax.rem(my_w + i, wafers) for i in range(wafers)]
-    others = s_peers[1:]
-
-    def for_peers(act):
-        if total <= 64:
-            for s in range(spans):
-                for w in range(wafers):
-                    if w or s:
-                        act(w_peers[w], s_peers[s])
-        else:
-
-            def step(i, carry):
-                other = lax.rem(me + i, total)
-                act(lax.div(other, spans), lax.rem(other, spans))
-                return carry
-
-            lax.fori_loop(1, total, step, 0)
+
+    others = [lax.rem(my_s + i, spans) for i in range(1, spans)]
+    other_wafers = [lax.rem(my_w + i, wafers) for i in range(1, wafers)]
 
     def own_start(s):
         return pl.multiple_of(s * span_len, span_len)
@@ -146,12 +138,13 @@
     )
     local = [pltpu.make_async_copy(a, b, local_sem.at[i]) for i, (a, b) in enumerate(pairs)]
     barrier = pltpu.get_barrier_semaphore()
-    for_peers(
-        lambda w, s: pl.semaphore_signal(barrier, inc=1, device_id=(w, s), device_id_type=MESH)
-    )
+    for s in others:
+        pl.semaphore_signal(barrier, inc=1, device_id=(my_w, s), device_id_type=MESH)
+    for w in other_wafers:
+        pl.semaphore_signal(barrier, inc=1, device_id=(w, my_s), device_id_type=MESH)
     for copy in local:
         copy.start()
-    pl.semaphore_wait(barrier, total - 1)
+    pl.semaphore_wait(barrier, spans + wafers - 2)
 
     def to_span(src, dst, which, s):
         pltpu.make_async_remote_copy(
@@ -167,7 +160,7 @@
         to_span(ts_ref.at[:, pl.ds(own_start(s), span_len)], ts_rx.at[my_s], 0, s)
     local[0].wait()
     templates = tm_ref[...]
-    gr_rx[my_s] = dot_nt(templates, templates)
+    gr_rx[my_s] = pack(dot_nt(templates, templates))
     for s in others:
         to_span(gr_rx.at[my_s], gr_rx.at[my_s], 1, s)
 
@@ -230,16 +223,16 @@
         ts_all[s * det_dev : (s + 1) * det_dev, :] = ts_rx[s]
     stream = ts_all[...]
     cleaned = stream - dot_nn(same_line, stream) * (NGROUP / det_w)
-    pj_rx[my_s] = dot_nt(cleaned, templates)
+    pj_rx[my_s] = pack(dot_nt(cleaned, templates))
     for s in others:
         to_span(pj_rx.at[my_s], pj_rx.at[my_s], 2, s)
 
     span_wait(gr_rx, span_recv, 1)
-    inverse = inverse_spd(jnp.sum(gr_rx[...], axis=0))
+    inverse = inverse_spd(unpack(jnp.sum(gr_rx[...], axis=0)))
     solved = dot_nn(inverse, templates)
 
     span_wait(pj_rx, span_recv, 2)
-    projection = jnp.sum(pj_rx[...], axis=0)
+    projection = unpack(jnp.sum(pj_rx[...], axis=0))
     filtered = cleaned - dot_nn(projection, solved)
     val_ref[...] = (sw_ref[...] * filtered).astype(BF16).astype(F32)
 
@@ -258,25 +251,27 @@
     else:
         part = lax.fori_loop(0, groups, bin_group, part)
 
-    wide = jnp.concatenate([part[q * hits : (q + 1) * hits, :] for q in range(2 * wafers)], axis=1)
-    out = dot_selected(selector, wide)
     for q in range(wafers):
-        for o in range(spans):
-            for m in range(2):
-                start = (m * wafers + q) * pix
-                tx[q * spans + o, m * CAP : (m + 1) * CAP] = out[
-                    o * CAP : (o + 1) * CAP, start : start + pix
-                ]
-
-    def send(w, s):
+        for m in range(2):
+            start = (m * wafers + q) * hits
+            wafer_tx[q, m * hits : (m + 1) * hits] = part[start : start + hits, :]
+    for w in other_wafers:
         pltpu.make_async_remote_copy(
-            src_ref=tx.at[w * spans + s], dst_ref=rx.at[me],
-            send_sem=tile_send, recv_sem=tile_recv,
-            device_id=(w, s), device_id_type=MESH,
+            src_ref=wafer_tx.at[w], dst_ref=wafer_rx.at[my_w],
+            send_sem=wafer_send, recv_sem=wafer_recv,
+            device_id=(w, my_s), device_id_type=MESH,
         ).start()
-
-    for_peers(send)
-    own = pltpu.make_async_copy(tx.at[me], rx.at[me], local_sem.at[0])
+    wafer_rx[my_w] = wafer_tx[my_w]
+    arrivals, departures = wafer_rx.at[pl.ds(0, wafers - 1)], wafer_tx.at[pl.ds(0, wafers - 1)]
+    pltpu.make_async_copy(arrivals, arrivals, wafer_recv).wait()
+    shared = jnp.sum(wafer_rx[...], axis=0)
+    out = dot_selected(selector, jnp.concatenate([shared[:hits, :], shared[hits:, :]], axis=1))
+    for o in range(spans):
+        for m in range(2):
+            tx[o, m * CAP : (m + 1) * CAP] = out[o * CAP : (o + 1) * CAP, m * pix : (m + 1) * pix]
+    for s in others:
+        to_span(tx.at[s], rx.at[my_s], 3, s)
+    own = pltpu.make_async_copy(tx.at[my_s], rx.at[my_s], local_sem.at[0])
     own.start()
 
     mine = (iota((det_dev, det_w), 1) == iota((det_dev, det_w), 0) + my_s * det_dev).astype(F32)
@@ -287,13 +282,13 @@
         span_wait(buffer, span_send, which)
     own.wait()
     fit.wait()
-    arrivals, departures = rx.at[pl.ds(0, total - 1)], tx.at[pl.ds(0, total - 1)]
-    pltpu.make_async_copy(departures, departures, tile_send).wait()
-    pltpu.make_async_copy(arrivals, arrivals, tile_recv).wait()
+    pltpu.make_async_copy(departures, departures, wafer_send).wait()
+    span_wait(tx, span_send, 3)
+    span_wait(rx, span_recv, 3)
 
 
 def collect(
-    wafers, spans, rx_hbm, fit_hbm, ht_hbm, fit_out, rhs_ref, wgt_ref, rx, ht_ref, sems
+    rx_hbm, fit_hbm, ht_hbm, fit_out, rhs_ref, wgt_ref, rx, ht_ref, sems
 ):
     arrivals = pltpu.make_async_copy(rx_hbm, rx, sems.at[0])
     listing = pltpu.make_async_copy(ht_hbm, ht_ref, sems.at[1])
@@ -314,10 +309,8 @@
     row_iota = iota((TILE_OWN, pix), 0).astype(F32)
     sums = [jnp.zeros((TILE_OWN, pix), F32) for m in range(2)]
     arrivals.wait()
-    for s in range(spans):
+    for s in range(rx.shape[0]):
         arrived = rx[s]
-        for w in range(1, wafers):
-            arrived = arrived + rx[w * spans + s]
         for k in range(CAP):
             here = row_iota == landing[k][s : s + 1, :]
             for m in range(2):
@@ -334,7 +327,6 @@
     nt, span_len = templates.shape
     det_w = pointing.shape[0]
     pix = TILE // wafers
-    total = wafers * spans
     vmem = pl.BlockSpec(memory_space=pltpu.VMEM)
     anywhere = pl.BlockSpec(memory_space=pl.ANY)
     fit_shape = jax.ShapeDtypeStruct((det_dev, nt), F32)
@@ -343,7 +335,7 @@
     groups = det_w // ROWS
     fit, tiles = pl.pallas_call(
         functools.partial(kernel, wafers, spans),
-        out_shape=(fit_shape, jax.ShapeDtypeStruct((total, 2 * CAP, pix), F32)),
+        out_shape=(fit_shape, jax.ShapeDtypeStruct((spans, 2 * CAP, pix), F32)),
         in_specs=[anywhere] * 8,
         out_specs=(anywhere,) * 2,
         scratch_shapes=[
@@ -356,16 +348,18 @@
             pltpu.VMEM(hit_tiles.shape, jnp.int32),
             pltpu.VMEM((spans, det_dev, span_len), F32),
             pltpu.VMEM((det_w, span_len), F32),
-            pltpu.VMEM((spans, nt, nt), F32),
-            pltpu.VMEM((spans, det_w, nt), F32),
+            pltpu.VMEM((spans, nt // 2, 2 * nt), F32),
+            pltpu.VMEM((spans, det_w // 2, 2 * nt), F32),
             pltpu.VMEM((det_w, span_len), F32),
             pltpu.VMEM((det_w, span_len), F32),
             pltpu.VMEM((groups, pix, ROWS * span_len), BF16),
             pltpu.VMEM((groups if groups <= 8 else 1, wafers * hits, ROWS * span_len), BF16),
-            pltpu.VMEM((total, 2 * CAP, pix), F32),
+            pltpu.VMEM((wafers, 2 * hits, pix), F32),
+            pltpu.VMEM((wafers, 2 * hits, pix), F32),
+            pltpu.VMEM((spans, 2 * CAP, pix), F32),
             pltpu.VMEM((det_dev, nt), F32),
-            pltpu.SemaphoreType.DMA((3,)),
-            pltpu.SemaphoreType.DMA((3,)),
+            pltpu.SemaphoreType.DMA((4,)),
+            pltpu.SemaphoreType.DMA((4,)),
             pltpu.SemaphoreType.DMA,
             pltpu.SemaphoreType.DMA,
             pltpu.SemaphoreType.DMA((8,)),
@@ -378,12 +372,12 @@
         cut_start.reshape(1, det_w), cut_len.reshape(1, det_w), pointing, hit_tiles,
     )
     return pl.pallas_call(
-        functools.partial(collect, wafers, spans),
+        collect,
         out_shape=(fit_shape, map_shape, map_shape),
         in_specs=[anywhere] * 3,
         out_specs=(anywhere, vmem, vmem),
         scratch_shapes=[
-            pltpu.VMEM((total, 2 * CAP, pix), F32),
+            pltpu.VMEM((spans, 2 * CAP, pix), F32),
             pltpu.VMEM(hit_tiles.shape, jnp.int32),
             pltpu.SemaphoreType.DMA((3,)),
         ],

time: 28.4 us -> 26.2 us (0.923)
  Pallas kernels: 27.6 us -> 25.3 us
    pallas_call x1, Pallas kernels: 25.8 us -> 23.5 us  [body(): pl.pallas_call(functools.partial(kernel, wafers, spans), out_shape=(fit_s...]
where the time goes in v4:
time: 26.2 us; the launch traced here: 26 us
  Pallas kernels  25.3 us (97%)
  between operations  0.64 us (2%)
    pallas_call x1, Pallas kernels, body(): pl.pallas_call(functools.partial(kernel, wafers, spans), out_shape=(fit_s...  23.5 us
    pallas_call x1, Pallas kernels, body(): pl.pallas_call(collect, out_shape=(fit_shape, map_shape, map_shape), in_s...  1.82 us

profile of v4, /device:TPU:0, one launch (start us, length us, event | category | flops | bytes accessed | tf_op | source)
XLA Modules:
  0.0 26.0 jit_solution(18192202251359422394)
XLA Ops:
  0.6 23.5 %shard_map.103 = (f32[6,64]{1,0:T(8,128)}, f32[8,4,128]{2,1,0:T(4,128)}) custom-call(f32[6,2048]{1,0:T(8,128)} %ts_ref.1, f32[64,256]{1,0:T(8,128)} %tm_hbm.1, s32[1,48]{1,0:T(1,128)} %bitcast.4, f32[1,48]{1,0:T(1,128)} %bitcast.5, s32[1,48]{1,0:T(1,128)} %bitcast.6, s32[1,48]{1,0:T(1,128)} %bitcast.7, s32[48,256]{1,0:T(8,128)} %pt_hbm.1, s32[8,8]{1,0:T(8,128)} %ht_hbm.3), custom_call_target="tpu_custom_call" | custom-call | tf_op jit(solution)/shard_map/pallas_call | solution.py:336
  24.2 1.8 %shard_map.104 = (f32[6,64]{1,0:T(8,128)}, f32[8,128]{1,0:T(8,128)}, f32[8,128]{1,0:T(8,128)}) custom-call(f32[8,4,128]{2,1,0:T(4,128)} %get-tuple-element.5.rx_hbm, f32[6,64]{1,0:T(8,128)} %get-tuple-element.6.fit_hbm, s32[8,8]{1,0:T(8,128)} %ht_hbm.3), custom_call_target="tpu_custom_call" | custom-call | tf_op jit(solution)/shard_map/pallas_call | solution.py:374

commit v5 on v4

--- a/solution.py
+++ b/solution.py
@@ -52,6 +52,12 @@
 def log2(value):
     assert value & (value - 1) == 0
     return value.bit_length() - 1
+
+
+def reciprocal(x):
+    guess = pl.reciprocal(x, approx=True)
+    guess = guess * (2.0 - x * guess)
+    return guess * (2.0 - x * guess)
 
 
 def inverse_spd(gram):
@@ -73,13 +79,16 @@
         columns = list(spread[p])
         for k in range(ROWS):
             pivot = columns[k]
-            scale = 1.0 / pivot[k : k + 1, :]
             here = row_of == k
-            top = panel[k : k + 1, :] * scale
-            panel = jnp.where(here, top, panel - pivot * top)
+            scale = reciprocal(jnp.broadcast_to(pivot[k : k + 1, :], (ROWS, wide)))
+
+            def swept(block):
+                top = block[k : k + 1, :]
+                return jnp.where(here, 0.0, block) - jnp.where(here, -top, pivot * top) * scale
+
+            panel = swept(panel)
             for c in range(k + 1, ROWS):
-                top = columns[c][k : k + 1, :] * scale
-                columns[c] = jnp.where(here, top, columns[c] - pivot * top)
+                columns[c] = swept(columns[c])
         for b in range(len(blocks)):
             if b == p:
                 blocks[b] = panel
@@ -113,9 +122,9 @@
 def kernel(
     wafers, spans,
     ts_ref, tm_hbm, bg_hbm, dw_hbm, cs_hbm, cl_hbm, pt_hbm, ht_hbm,
-    fit_hbm, rx,
+    fit_hbm, rx, marks_hbm,
     tm_ref, bg_ref, dw_ref, cs_ref, cl_ref, pt_ref, ht_ref,
-    ts_rx, ts_all, gr_rx, pj_rx, sw_ref, val_ref, hot_ref, left_ref, wafer_tx, wafer_rx, tx, fit_ref,
+    ts_rx, ts_all, gr_rx, pj_rx, sw_ref, val_ref, hot_ref, left_ref, wafer_tx, wafer_rx, tx, fit_ref, marks_ref,
     span_send, span_recv, wafer_send, wafer_recv, local_sem,
 ):
     det_dev = ts_ref.shape[0]
@@ -144,6 +153,9 @@
         pl.semaphore_signal(barrier, inc=1, device_id=(w, my_s), device_id_type=MESH)
     for copy in local:
         copy.start()
+    local[0].wait()
+    templates = tm_ref[...]
+    gr_rx[my_s] = pack(dot_nt(templates, templates))
     pl.semaphore_wait(barrier, spans + wafers - 2)
 
     def to_span(src, dst, which, s):
@@ -158,9 +170,6 @@
 
     for s in others:
         to_span(ts_ref.at[:, pl.ds(own_start(s), span_len)], ts_rx.at[my_s], 0, s)
-    local[0].wait()
-    templates = tm_ref[...]
-    gr_rx[my_s] = pack(dot_nt(templates, templates))
     for s in others:
         to_span(gr_rx.at[my_s], gr_rx.at[my_s], 1, s)
 
@@ -171,6 +180,14 @@
     own_code = jnp.sum(jnp.where(iota(code.shape, 0) == my_s, code, 0.0), axis=0, keepdims=True)
     slots = spans * CAP
     selector = (own_code == iota((slots, hits), 0).astype(F32)).astype(BF16)
+
+    place_of = (ht_ref[...] - (my_s * TILE_OWN - 1)).astype(F32)
+    for k in range(CAP):
+        mine = code == (my_s * CAP + k).astype(F32)
+        landing = jnp.sum(jnp.where(mine, place_of, 0.0), axis=1, keepdims=True) - 1.0
+        marks_ref[k] = jnp.broadcast_to(landing, (spans, pix))
+    marks = pltpu.make_async_copy(marks_ref, marks_hbm, local_sem.at[2])
+    marks.start()
 
     time = (iota((det_w, span_len), 1) + my_s * span_len).astype(F32)
     cut_start = to_column(cs_ref[...])
@@ -216,13 +233,13 @@
 
     lax.fori_loop(0, groups, prepare, 0, unroll=2)
 
-    same_line = (bg_ref[...].astype(F32) == to_column(bg_ref[...])).astype(F32)
+    same_line = (bg_ref[...].astype(F32) == to_column(bg_ref[...])).astype(BF16)
     local[1].wait()
     span_wait(ts_rx, span_recv, 0)
     for s in range(spans):
         ts_all[s * det_dev : (s + 1) * det_dev, :] = ts_rx[s]
     stream = ts_all[...]
-    cleaned = stream - dot_nn(same_line, stream) * (NGROUP / det_w)
+    cleaned = stream - dot_selected(same_line, stream) * (NGROUP / det_w)
     pj_rx[my_s] = pack(dot_nt(cleaned, templates))
     for s in others:
         to_span(pj_rx.at[my_s], pj_rx.at[my_s], 2, s)
@@ -282,37 +299,27 @@
         span_wait(buffer, span_send, which)
     own.wait()
     fit.wait()
+    marks.wait()
     pltpu.make_async_copy(departures, departures, wafer_send).wait()
     span_wait(tx, span_send, 3)
     span_wait(rx, span_recv, 3)
 
 
-def collect(
-    rx_hbm, fit_hbm, ht_hbm, fit_out, rhs_ref, wgt_ref, rx, ht_ref, sems
-):
+def collect(rx_hbm, fit_hbm, marks_hbm, fit_out, rhs_ref, wgt_ref, rx, marks_ref, sems):
     arrivals = pltpu.make_async_copy(rx_hbm, rx, sems.at[0])
-    listing = pltpu.make_async_copy(ht_hbm, ht_ref, sems.at[1])
+    marks = pltpu.make_async_copy(marks_hbm, marks_ref, sems.at[1])
     fit = pltpu.make_async_copy(fit_hbm, fit_out, sems.at[2])
-    listing.start()
+    marks.start()
     arrivals.start()
     fit.start()
-    my_s = lax.axis_index("span")
-    pix = rhs_ref.shape[1]
-    listing.wait()
-    listed = ht_ref[...]
-    code = slot_codes(listed)
-    place = (listed - (my_s * TILE_OWN - 1)).astype(F32)
-    landing = [
-        jnp.sum(jnp.where(code == (my_s * CAP + k).astype(F32), place, 0.0), axis=1, keepdims=True) - 1.0
-        for k in range(CAP)
-    ]
-    row_iota = iota((TILE_OWN, pix), 0).astype(F32)
-    sums = [jnp.zeros((TILE_OWN, pix), F32) for m in range(2)]
+    row_iota = iota(rhs_ref.shape, 0).astype(F32)
+    sums = [jnp.zeros(rhs_ref.shape, F32) for m in range(2)]
+    marks.wait()
     arrivals.wait()
     for s in range(rx.shape[0]):
         arrived = rx[s]
         for k in range(CAP):
-            here = row_iota == landing[k][s : s + 1, :]
+            here = row_iota == marks_ref[k, s : s + 1, :]
             for m in range(2):
                 row = m * CAP + k
                 sums[m] = sums[m] + jnp.where(here, arrived[row : row + 1, :], 0.0)
@@ -333,11 +340,12 @@
     map_shape = jax.ShapeDtypeStruct((TILE_OWN, pix), F32)
     hits = hit_tiles.shape[1]
     groups = det_w // ROWS
-    fit, tiles = pl.pallas_call(
+    marks_shape = (CAP, spans, pix)
+    fit, tiles, marks = pl.pallas_call(
         functools.partial(kernel, wafers, spans),
-        out_shape=(fit_shape, jax.ShapeDtypeStruct((spans, 2 * CAP, pix), F32)),
+        out_shape=(fit_shape, jax.ShapeDtypeStruct((spans, 2 * CAP, pix), F32), jax.ShapeDtypeStruct(marks_shape, F32)),
         in_specs=[anywhere] * 8,
-        out_specs=(anywhere,) * 2,
+        out_specs=(anywhere,) * 3,
         scratch_shapes=[
             pltpu.VMEM((nt, span_len), F32),
             pltpu.VMEM((1, det_w), jnp.int32),
@@ -358,6 +366,7 @@
             pltpu.VMEM((wafers, 2 * hits, pix), F32),
             pltpu.VMEM((spans, 2 * CAP, pix), F32),
             pltpu.VMEM((det_dev, nt), F32),
+            pltpu.VMEM(marks_shape, F32),
             pltpu.SemaphoreType.DMA((4,)),
             pltpu.SemaphoreType.DMA((4,)),
             pltpu.SemaphoreType.DMA,
@@ -378,10 +387,10 @@
         out_specs=(anywhere, vmem, vmem),
         scratch_shapes=[
             pltpu.VMEM((spans, 2 * CAP, pix), F32),
-            pltpu.VMEM(hit_tiles.shape, jnp.int32),
+            pltpu.VMEM(marks_shape, F32),
             pltpu.SemaphoreType.DMA((3,)),
         ],
-    )(tiles, fit, hit_tiles)
+    )(tiles, fit, marks)
 
 
 def solution(mesh):

time: 26.2 us -> 26.4 us (level)
  no operation moved by 1% of the time
where the time goes in v5:
time: 26.4 us; the launch traced here: 26.1 us
  Pallas kernels  25.5 us (97%)
  between operations  0.64 us (2%)
    pallas_call x1, Pallas kernels, body(): pl.pallas_call(functools.partial(kernel, wafers, spans), out_shape=(fit_s...  23.7 us
    pallas_call x1, Pallas kernels, body(): pl.pallas_call(collect, out_shape=(fit_shape, map_shape, map_shape), in_s...  1.82 us

profile of v5, /device:TPU:0, one launch (start us, length us, event | category | flops | bytes accessed | tf_op | source)
XLA Modules:
  0.0 26.1 jit_solution(11426426348029774971)
XLA Ops:
  0.6 23.7 %shard_map.103 = (f32[6,64]{1,0:T(8,128)}, f32[8,4,128]{2,1,0:T(4,128)}, f32[2,8,128]{2,1,0:T(8,128)}) custom-call(f32[6,2048]{1,0:T(8,128)} %ts_ref.1, f32[64,256]{1,0:T(8,128)} %tm_hbm.1, s32[1,48]{1,0:T(1,128)} %bitcast.4, f32[1,48]{1,0:T(1,128)} %bitcast.5, s32[1,48]{1,0:T(1,128)} %bitcast.6, s32[1,48]{1,0:T(1,128)} %bitcast.7, s32[48,256]{1,0:T(8,128)} %pt_hbm.1, ...), custom_call_target="tpu_custom_call" | custom-call | tf_op jit(solution)/shard_map/pallas_call | solution.py:344
  24.3 1.8 %shard_map.104 = (f32[6,64]{1,0:T(8,128)}, f32[8,128]{1,0:T(8,128)}, f32[8,128]{1,0:T(8,128)}) custom-call(f32[8,4,128]{2,1,0:T(4,128)} %get-tuple-element.6.rx_hbm, f32[6,64]{1,0:T(8,128)} %get-tuple-element.7.fit_hbm, f32[2,8,128]{2,1,0:T(8,128)} %get-tuple-element.8.marks_hbm), custom_call_target="tpu_custom_call" | custom-call | tf_op jit(solution)/shard_map/pallas_call | solution.py:383

commit v6 on v5

--- a/solution.py
+++ b/solution.py
@@ -60,11 +60,11 @@
     return guess * (2.0 - x * guess)
 
 
-def inverse_spd(gram):
-    size = gram.shape[0]
-    wide = 2 * size
-    eye = (iota((size, size), 0) == iota((size, size), 1)).astype(F32)
-    joined = jnp.concatenate([eye, gram], axis=1)
+def inverse_spd(twice):
+    size, wide = twice.shape
+    lane = iota(twice.shape, 1)
+    eye = (iota(twice.shape, 0) == lane).astype(F32)
+    joined = jnp.where(lane < size, eye, twice)
     blocks = [joined[ROWS * b : ROWS * (b + 1), :] for b in range(size // ROWS)]
     row_of = iota((ROWS, wide), 0)
     for p in range(size // ROWS):
@@ -124,7 +124,7 @@
     ts_ref, tm_hbm, bg_hbm, dw_hbm, cs_hbm, cl_hbm, pt_hbm, ht_hbm,
     fit_hbm, rx, marks_hbm,
     tm_ref, bg_ref, dw_ref, cs_ref, cl_ref, pt_ref, ht_ref,
-    ts_rx, ts_all, gr_rx, pj_rx, sw_ref, val_ref, hot_ref, left_ref, wafer_tx, wafer_rx, tx, fit_ref, marks_ref,
+    ts_rx, ts_all, gr_tx, gr_rx, gr_all, pj_rx, sw_ref, val_ref, hot_ref, left_ref, wafer_tx, wafer_rx, tx, fit_ref, marks_ref,
     span_send, span_recv, wafer_send, wafer_recv, local_sem,
 ):
     det_dev = ts_ref.shape[0]
@@ -155,7 +155,11 @@
         copy.start()
     local[0].wait()
     templates = tm_ref[...]
-    gr_rx[my_s] = pack(dot_nt(templates, templates))
+    twice = dot_nt(templates, jnp.concatenate([templates, templates], axis=0))
+    piece = nt // spans
+    for s in range(spans):
+        gr_tx[s] = twice[s * piece : (s + 1) * piece, :]
+    gr_rx[my_s] = gr_tx[my_s]
     pl.semaphore_wait(barrier, spans + wafers - 2)
 
     def to_span(src, dst, which, s):
@@ -171,7 +175,7 @@
     for s in others:
         to_span(ts_ref.at[:, pl.ds(own_start(s), span_len)], ts_rx.at[my_s], 0, s)
     for s in others:
-        to_span(gr_rx.at[my_s], gr_rx.at[my_s], 1, s)
+        to_span(gr_tx.at[s], gr_rx.at[my_s], 1, s)
 
     for copy in local[2:]:
         copy.wait()
@@ -234,6 +238,10 @@
     lax.fori_loop(0, groups, prepare, 0, unroll=2)
 
     same_line = (bg_ref[...].astype(F32) == to_column(bg_ref[...])).astype(BF16)
+    span_wait(gr_rx, span_recv, 1)
+    gr_all[my_s] = jnp.sum(gr_rx[...], axis=0)
+    for s in others:
+        to_span(gr_all.at[my_s], gr_all.at[my_s], 4, s)
     local[1].wait()
     span_wait(ts_rx, span_recv, 0)
     for s in range(spans):
@@ -244,8 +252,8 @@
     for s in others:
         to_span(pj_rx.at[my_s], pj_rx.at[my_s], 2, s)
 
-    span_wait(gr_rx, span_recv, 1)
-    inverse = inverse_spd(unpack(jnp.sum(gr_rx[...], axis=0)))
+    span_wait(gr_all, span_recv, 4)
+    inverse = inverse_spd(jnp.concatenate([gr_all[s] for s in range(spans)], axis=0))
     solved = dot_nn(inverse, templates)
 
     span_wait(pj_rx, span_recv, 2)
@@ -295,7 +303,7 @@
     fit_ref[...] = dot_nn(dot_nn(mine, projection), inverse)
     fit = pltpu.make_async_copy(fit_ref, fit_hbm, local_sem.at[1])
     fit.start()
-    for which, buffer in enumerate((ts_rx, gr_rx, pj_rx)):
+    for which, buffer in ((0, ts_rx), (1, gr_rx), (2, pj_rx), (4, gr_all)):
         span_wait(buffer, span_send, which)
     own.wait()
     fit.wait()
@@ -356,7 +364,9 @@
             pltpu.VMEM(hit_tiles.shape, jnp.int32),
             pltpu.VMEM((spans, det_dev, span_len), F32),
             pltpu.VMEM((det_w, span_len), F32),
-            pltpu.VMEM((spans, nt // 2, 2 * nt), F32),
+            pltpu.VMEM((spans, nt // spans, 2 * nt), F32),
+            pltpu.VMEM((spans, nt // spans, 2 * nt), F32),
+            pltpu.VMEM((spans, nt // spans, 2 * nt), F32),
             pltpu.VMEM((spans, det_w // 2, 2 * nt), F32),
             pltpu.VMEM((det_w, span_len), F32),
             pltpu.VMEM((det_w, span_len), F32),
@@ -367,8 +377,8 @@
             pltpu.VMEM((spans, 2 * CAP, pix), F32),
             pltpu.VMEM((det_dev, nt), F32),
             pltpu.VMEM(marks_shape, F32),
-            pltpu.SemaphoreType.DMA((4,)),
-            pltpu.SemaphoreType.DMA((4,)),
+            pltpu.SemaphoreType.DMA((5,)),
+            pltpu.SemaphoreType.DMA((5,)),
             pltpu.SemaphoreType.DMA,
             pltpu.SemaphoreType.DMA,
             pltpu.SemaphoreType.DMA((8,)),

time: 26.4 us -> 27.8 us (1.053)
  Pallas kernels: 25.5 us -> 27 us
    pallas_call x1, Pallas kernels: 23.7 us -> 25.1 us  [body(): pl.pallas_call(functools.partial(kernel, wafers, spans), out_shape=(fit_s...]
where the time goes in v6:
time: 27.8 us; the launch traced here: 27.6 us
  Pallas kernels  27 us (97%)
  between operations  0.64 us (2%)
    pallas_call x1, Pallas kernels, body(): pl.pallas_call(functools.partial(kernel, wafers, spans), out_shape=(fit_s...  25.1 us
    pallas_call x1, Pallas kernels, body(): pl.pallas_call(collect, out_shape=(fit_shape, map_shape, map_shape), in_s...  1.82 us

profile of v6, /device:TPU:0, one launch (start us, length us, event | category | flops | bytes accessed | tf_op | source)
XLA Modules:
  0.0 27.6 jit_solution(7234501883090226973)
XLA Ops:
  0.6 25.1 %shard_map.103 = (f32[6,64]{1,0:T(8,128)}, f32[8,4,128]{2,1,0:T(4,128)}, f32[2,8,128]{2,1,0:T(8,128)}) custom-call(f32[6,2048]{1,0:T(8,128)} %ts_ref.1, f32[64,256]{1,0:T(8,128)} %tm_hbm.1, s32[1,48]{1,0:T(1,128)} %bitcast.4, f32[1,48]{1,0:T(1,128)} %bitcast.5, s32[1,48]{1,0:T(1,128)} %bitcast.6, s32[1,48]{1,0:T(1,128)} %bitcast.7, s32[48,256]{1,0:T(8,128)} %pt_hbm.1, ...), custom_call_target="tpu_custom_call" | custom-call | tf_op jit(solution)/shard_map/pallas_call | solution.py:352
  25.8 1.8 %shard_map.104 = (f32[6,64]{1,0:T(8,128)}, f32[8,128]{1,0:T(8,128)}, f32[8,128]{1,0:T(8,128)}) custom-call(f32[8,4,128]{2,1,0:T(4,128)} %get-tuple-element.6.rx_hbm, f32[6,64]{1,0:T(8,128)} %get-tuple-element.7.fit_hbm, f32[2,8,128]{2,1,0:T(8,128)} %get-tuple-element.8.marks_hbm), custom_call_target="tpu_custom_call" | custom-call | tf_op jit(solution)/shard_map/pallas_call | solution.py:393

commit v7 on v4

--- a/solution.py
+++ b/solution.py
@@ -179,14 +179,30 @@
     sw_ref[...] = jnp.where(inside, 0.0, to_column(dw_ref[...])).astype(BF16).astype(F32)
 
     coarse_count = wafers * hits
-    coarse_iota = iota((coarse_count, span_len), 0)
-    fine_iota = iota((pix, span_len), 0)
+    assert max(coarse_count, pix) <= 256
+    pair = 2 * ROWS
+    nought = jnp.zeros((pair, span_len), BF16)
+    unit = jnp.ones((pair, span_len), BF16)
+
+    def numbered(count):
+        rows = iota((pair, span_len), 0).astype(F32)
+        return [(rows + float(start)).astype(BF16) for start in range(0, count, pair)]
+
+    coarse_iota, fine_iota = numbered(coarse_count), numbered(pix)
+
+    def spread(row):
+        return jnp.broadcast_to(row, (pair, span_len)).astype(BF16)
+
+    def one_hot(numbers, index, value):
+        index = spread(index)
+        return jnp.concatenate([jnp.where(block == index, value, nought) for block in numbers], axis=0)
 
     def shifted(x, amount):
         return lax.shift_right_logical(x, jnp.full(x.shape, amount, jnp.int32))
 
     def coarse_of(points):
-        return (shifted(points, log2(pix)) & (wafers - 1)) * hits + shifted(points, log2(TILE))
+        coarse = (shifted(points, log2(pix)) & (wafers - 1)) * hits + shifted(points, log2(TILE))
+        return coarse.astype(F32)
 
     groups = det_w // ROWS
     keep_left = left_ref.shape[0] == groups
@@ -194,7 +210,7 @@
     def place(coarse, values):
         return jnp.concatenate(
             [
-                jnp.where(coarse_iota == coarse[r : r + 1, :], values[r : r + 1, :], 0.0).astype(BF16)
+                one_hot(coarse_iota, coarse[r : r + 1, :], spread(values[r : r + 1, :]))
                 for r in range(ROWS)
             ],
             axis=1,
@@ -205,10 +221,9 @@
 
     def prepare(g, carry):
         points = pt_ref[rows_of(g), :]
-        fine = points & (pix - 1)
+        fine = (points & (pix - 1)).astype(F32)
         hot_ref[g] = jnp.concatenate(
-            [jnp.where(fine_iota == fine[r : r + 1, :], 1.0, 0.0).astype(BF16) for r in range(ROWS)],
-            axis=1,
+            [one_hot(fine_iota, fine[r : r + 1, :], unit) for r in range(ROWS)], axis=1
         )
         if keep_left:
             left_ref[g] = place(coarse_of(points), sw_ref[rows_of(g), :])

time: 26.2 us -> 26.1 us (level)
  no operation moved by 1% of the time
where the time goes in v7:
time: 26.1 us; the launch traced here: 26 us
  Pallas kernels  25.3 us (97%)
  between operations  0.64 us (2%)
    pallas_call x1, Pallas kernels, body(): pl.pallas_call(functools.partial(kernel, wafers, spans), out_shape=(fit_s...  23.5 us
    pallas_call x1, Pallas kernels, body(): pl.pallas_call(collect, out_shape=(fit_shape, map_shape, map_shape), in_s...  1.82 us

profile of v7, /device:TPU:0, one launch (start us, length us, event | category | flops | bytes accessed | tf_op | source)
XLA Modules:
  0.0 26.0 jit_solution(3391327542721749669)
XLA Ops:
  0.6 23.5 %shard_map.103 = (f32[6,64]{1,0:T(8,128)}, f32[8,4,128]{2,1,0:T(4,128)}) custom-call(f32[6,2048]{1,0:T(8,128)} %ts_ref.1, f32[64,256]{1,0:T(8,128)} %tm_hbm.1, s32[1,48]{1,0:T(1,128)} %bitcast.4, f32[1,48]{1,0:T(1,128)} %bitcast.5, s32[1,48]{1,0:T(1,128)} %bitcast.6, s32[1,48]{1,0:T(1,128)} %bitcast.7, s32[48,256]{1,0:T(8,128)} %pt_hbm.1, s32[8,8]{1,0:T(8,128)} %ht_hbm.3), custom_call_target="tpu_custom_call" | custom-call | tf_op jit(solution)/shard_map/pallas_call | solution.py:351
  24.1 1.8 %shard_map.104 = (f32[6,64]{1,0:T(8,128)}, f32[8,128]{1,0:T(8,128)}, f32[8,128]{1,0:T(8,128)}) custom-call(f32[8,4,128]{2,1,0:T(4,128)} %get-tuple-element.5.rx_hbm, f32[6,64]{1,0:T(8,128)} %get-tuple-element.6.fit_hbm, s32[8,8]{1,0:T(8,128)} %ht_hbm.3), custom_call_target="tpu_custom_call" | custom-call | tf_op jit(solution)/shard_map/pallas_call | solution.py:389

commit v8 on v5

--- a/solution.py
+++ b/solution.py
@@ -153,9 +153,6 @@
         pl.semaphore_signal(barrier, inc=1, device_id=(w, my_s), device_id_type=MESH)
     for copy in local:
         copy.start()
-    local[0].wait()
-    templates = tm_ref[...]
-    gr_rx[my_s] = pack(dot_nt(templates, templates))
     pl.semaphore_wait(barrier, spans + wafers - 2)
 
     def to_span(src, dst, which, s):
@@ -170,6 +167,9 @@
 
     for s in others:
         to_span(ts_ref.at[:, pl.ds(own_start(s), span_len)], ts_rx.at[my_s], 0, s)
+    local[0].wait()
+    templates = tm_ref[...]
+    gr_rx[my_s] = pack(dot_nt(templates, templates))
     for s in others:
         to_span(gr_rx.at[my_s], gr_rx.at[my_s], 1, s)
 
@@ -196,14 +196,30 @@
     sw_ref[...] = jnp.where(inside, 0.0, to_column(dw_ref[...])).astype(BF16).astype(F32)
 
     coarse_count = wafers * hits
-    coarse_iota = iota((coarse_count, span_len), 0)
-    fine_iota = iota((pix, span_len), 0)
+    assert max(coarse_count, pix) <= 256
+    pair = 2 * ROWS
+    nought = jnp.zeros((pair, span_len), BF16)
+    unit = jnp.ones((pair, span_len), BF16)
+
+    def numbered(count):
+        rows = iota((pair, span_len), 0).astype(F32)
+        return [(rows + float(start)).astype(BF16) for start in range(0, count, pair)]
+
+    coarse_iota, fine_iota = numbered(coarse_count), numbered(pix)
+
+    def spread(row):
+        return jnp.broadcast_to(row, (pair, span_len)).astype(BF16)
+
+    def one_hot(numbers, index, value):
+        index = spread(index)
+        return jnp.concatenate([jnp.where(block == index, value, nought) for block in numbers], axis=0)
 
     def shifted(x, amount):
         return lax.shift_right_logical(x, jnp.full(x.shape, amount, jnp.int32))
 
     def coarse_of(points):
-        return (shifted(points, log2(pix)) & (wafers - 1)) * hits + shifted(points, log2(TILE))
+        coarse = (shifted(points, log2(pix)) & (wafers - 1)) * hits + shifted(points, log2(TILE))
+        return coarse.astype(F32)
 
     groups = det_w // ROWS
     keep_left = left_ref.shape[0] == groups
@@ -211,7 +227,7 @@
     def place(coarse, values):
         return jnp.concatenate(
             [
-                jnp.where(coarse_iota == coarse[r : r + 1, :], values[r : r + 1, :], 0.0).astype(BF16)
+                one_hot(coarse_iota, coarse[r : r + 1, :], spread(values[r : r + 1, :]))
                 for r in range(ROWS)
             ],
             axis=1,
@@ -222,10 +238,9 @@
 
     def prepare(g, carry):
         points = pt_ref[rows_of(g), :]
-        fine = points & (pix - 1)
+        fine = (points & (pix - 1)).astype(F32)
         hot_ref[g] = jnp.concatenate(
-            [jnp.where(fine_iota == fine[r : r + 1, :], 1.0, 0.0).astype(BF16) for r in range(ROWS)],
-            axis=1,
+            [one_hot(fine_iota, fine[r : r + 1, :], unit) for r in range(ROWS)], axis=1
         )
         if keep_left:
             left_ref[g] = place(coarse_of(points), sw_ref[rows_of(g), :])

time: 26.4 us -> 26.3 us (level)
  no operation moved by 1% of the time
where the time goes in v8:
time: 26.3 us; the launch traced here: 26.1 us
  Pallas kernels  25.5 us (97%)
  between operations  0.64 us (2%)
    pallas_call x1, Pallas kernels, body(): pl.pallas_call(functools.partial(kernel, wafers, spans), out_shape=(fit_s...  23.6 us
    pallas_call x1, Pallas kernels, body(): pl.pallas_call(collect, out_shape=(fit_shape, map_shape, map_shape), in_s...  1.82 us

profile of v8, /device:TPU:0, one launch (start us, length us, event | category | flops | bytes accessed | tf_op | source)
XLA Modules:
  0.0 26.1 jit_solution(14226810593050025665)
XLA Ops:
  0.6 23.6 %shard_map.103 = (f32[6,64]{1,0:T(8,128)}, f32[8,4,128]{2,1,0:T(4,128)}, f32[2,8,128]{2,1,0:T(8,128)}) custom-call(f32[6,2048]{1,0:T(8,128)} %ts_ref.1, f32[64,256]{1,0:T(8,128)} %tm_hbm.1, s32[1,48]{1,0:T(1,128)} %bitcast.4, f32[1,48]{1,0:T(1,128)} %bitcast.5, s32[1,48]{1,0:T(1,128)} %bitcast.6, s32[1,48]{1,0:T(1,128)} %bitcast.7, s32[48,256]{1,0:T(8,128)} %pt_hbm.1, ...), custom_call_target="tpu_custom_call" | custom-call | tf_op jit(solution)/shard_map/pallas_call | solution.py:359
  24.3 1.8 %shard_map.104 = (f32[6,64]{1,0:T(8,128)}, f32[8,128]{1,0:T(8,128)}, f32[8,128]{1,0:T(8,128)}) custom-call(f32[8,4,128]{2,1,0:T(4,128)} %get-tuple-element.6.rx_hbm, f32[6,64]{1,0:T(8,128)} %get-tuple-element.7.fit_hbm, f32[2,8,128]{2,1,0:T(8,128)} %get-tuple-element.8.marks_hbm), custom_call_target="tpu_custom_call" | custom-call | tf_op jit(solution)/shard_map/pallas_call | solution.py:398

commit v9 on v7

--- a/solution.py
+++ b/solution.py
@@ -115,7 +115,7 @@
     ts_ref, tm_hbm, bg_hbm, dw_hbm, cs_hbm, cl_hbm, pt_hbm, ht_hbm,
     fit_hbm, rx,
     tm_ref, bg_ref, dw_ref, cs_ref, cl_ref, pt_ref, ht_ref,
-    ts_rx, ts_all, gr_rx, pj_rx, sw_ref, val_ref, hot_ref, left_ref, wafer_tx, wafer_rx, tx, fit_ref,
+    ts_rx, ts_all, gr_rx, pj_rx, sw_ref, val_ref, hot_ref, left_ref, tx, fit_ref,
     span_send, span_recv, wafer_send, wafer_recv, local_sem,
 ):
     det_dev = ts_ref.shape[0]
@@ -266,27 +266,26 @@
     else:
         part = lax.fori_loop(0, groups, bin_group, part)
 
+    wide = jnp.concatenate([part[q * hits : (q + 1) * hits, :] for q in range(2 * wafers)], axis=1)
+    out = dot_selected(selector, wide)
     for q in range(wafers):
-        for m in range(2):
-            start = (m * wafers + q) * hits
-            wafer_tx[q, m * hits : (m + 1) * hits] = part[start : start + hits, :]
-    for w in other_wafers:
-        pltpu.make_async_remote_copy(
-            src_ref=wafer_tx.at[w], dst_ref=wafer_rx.at[my_w],
-            send_sem=wafer_send, recv_sem=wafer_recv,
-            device_id=(w, my_s), device_id_type=MESH,
-        ).start()
-    wafer_rx[my_w] = wafer_tx[my_w]
-    arrivals, departures = wafer_rx.at[pl.ds(0, wafers - 1)], wafer_tx.at[pl.ds(0, wafers - 1)]
-    pltpu.make_async_copy(arrivals, arrivals, wafer_recv).wait()
-    shared = jnp.sum(wafer_rx[...], axis=0)
-    out = dot_selected(selector, jnp.concatenate([shared[:hits, :], shared[hits:, :]], axis=1))
-    for o in range(spans):
-        for m in range(2):
-            tx[o, m * CAP : (m + 1) * CAP] = out[o * CAP : (o + 1) * CAP, m * pix : (m + 1) * pix]
-    for s in others:
-        to_span(tx.at[s], rx.at[my_s], 3, s)
-    own = pltpu.make_async_copy(tx.at[my_s], rx.at[my_s], local_sem.at[0])
+        for o in range(spans):
+            for m in range(2):
+                start = (m * wafers + q) * pix
+                tx[q * spans + o, m * CAP : (m + 1) * CAP] = out[
+                    o * CAP : (o + 1) * CAP, start : start + pix
+                ]
+    me = my_w * spans + my_s
+    for w in other_wafers + [my_w]:
+        for s in others + [my_s]:
+            if w is my_w and s is my_s:
+                continue
+            pltpu.make_async_remote_copy(
+                src_ref=tx.at[w * spans + s], dst_ref=rx.at[me],
+                send_sem=wafer_send, recv_sem=wafer_recv,
+                device_id=(w, s), device_id_type=MESH,
+            ).start()
+    own = pltpu.make_async_copy(tx.at[me], rx.at[me], local_sem.at[0])
     own.start()
 
     mine = (iota((det_dev, det_w), 1) == iota((det_dev, det_w), 0) + my_s * det_dev).astype(F32)
@@ -297,9 +296,10 @@
         span_wait(buffer, span_send, which)
     own.wait()
     fit.wait()
+    total = wafers * spans
+    arrivals, departures = rx.at[pl.ds(0, total - 1)], tx.at[pl.ds(0, total - 1)]
     pltpu.make_async_copy(departures, departures, wafer_send).wait()
-    span_wait(tx, span_send, 3)
-    span_wait(rx, span_recv, 3)
+    pltpu.make_async_copy(arrivals, arrivals, wafer_recv).wait()
 
 
 def collect(
@@ -324,8 +324,11 @@
     row_iota = iota((TILE_OWN, pix), 0).astype(F32)
     sums = [jnp.zeros((TILE_OWN, pix), F32) for m in range(2)]
     arrivals.wait()
-    for s in range(rx.shape[0]):
+    spans = ht_ref.shape[0]
+    for s in range(spans):
         arrived = rx[s]
+        for w in range(1, rx.shape[0] // spans):
+            arrived = arrived + rx[w * spans + s]
         for k in range(CAP):
             here = row_iota == landing[k][s : s + 1, :]
             for m in range(2):
@@ -350,7 +353,7 @@
     groups = det_w // ROWS
     fit, tiles = pl.pallas_call(
         functools.partial(kernel, wafers, spans),
-        out_shape=(fit_shape, jax.ShapeDtypeStruct((spans, 2 * CAP, pix), F32)),
+        out_shape=(fit_shape, jax.ShapeDtypeStruct((wafers * spans, 2 * CAP, pix), F32)),
         in_specs=[anywhere] * 8,
         out_specs=(anywhere,) * 2,
         scratch_shapes=[
@@ -369,9 +372,7 @@
             pltpu.VMEM((det_w, span_len), F32),
             pltpu.VMEM((groups, pix, ROWS * span_len), BF16),
             pltpu.VMEM((groups if groups <= 8 else 1, wafers * hits, ROWS * span_len), BF16),
-            pltpu.VMEM((wafers, 2 * hits, pix), F32),
-            pltpu.VMEM((wafers, 2 * hits, pix), F32),
-            pltpu.VMEM((spans, 2 * CAP, pix), F32),
+            pltpu.VMEM((wafers * spans, 2 * CAP, pix), F32),
             pltpu.VMEM((det_dev, nt), F32),
             pltpu.SemaphoreType.DMA((4,)),
             pltpu.SemaphoreType.DMA((4,)),
@@ -392,7 +393,7 @@
         in_specs=[anywhere] * 3,
         out_specs=(anywhere, vmem, vmem),
         scratch_shapes=[
-            pltpu.VMEM((spans, 2 * CAP, pix), F32),
+            pltpu.VMEM((wafers * spans, 2 * CAP, pix), F32),
             pltpu.VMEM(hit_tiles.shape, jnp.int32),
             pltpu.SemaphoreType.DMA((3,)),
         ],

time: 26.1 us -> 24 us (0.920)
  Pallas kernels: 25.3 us -> 23.2 us
    pallas_call x1, Pallas kernels: 23.5 us -> 21.4 us  [body(): pl.pallas_call(functools.partial(kernel, wafers, spans), out_shape=(fit_s...]
where the time goes in v9:
time: 24 us; the launch traced here: 23.8 us
  Pallas kernels  23.2 us (97%)
  between operations  0.64 us (3%)
    pallas_call x1, Pallas kernels, body(): pl.pallas_call(functools.partial(kernel, wafers, spans), out_shape=(fit_s...  21.4 us
    pallas_call x1, Pallas kernels, body(): pl.pallas_call(collect, out_shape=(fit_shape, map_shape, map_shape), in_s...  1.82 us

profile of v9, /device:TPU:0, one launch (start us, length us, event | category | flops | bytes accessed | tf_op | source)
XLA Modules:
  0.0 23.8 jit_solution(950441439594367115)
XLA Ops:
  0.6 21.4 %shard_map.103 = (f32[6,64]{1,0:T(8,128)}, f32[32,4,128]{2,1,0:T(4,128)}) custom-call(f32[6,2048]{1,0:T(8,128)} %ts_ref.1, f32[64,256]{1,0:T(8,128)} %tm_hbm.1, s32[1,48]{1,0:T(1,128)} %bitcast.4, f32[1,48]{1,0:T(1,128)} %bitcast.5, s32[1,48]{1,0:T(1,128)} %bitcast.6, s32[1,48]{1,0:T(1,128)} %bitcast.7, s32[48,256]{1,0:T(8,128)} %pt_hbm.1, s32[8,8]{1,0:T(8,128)} %ht_hbm.3), custom_call_target="tpu_custom_call" | custom-call | tf_op jit(solution)/shard_map/pallas_call | solution.py:354
  22.0 1.8 %shard_map.104 = (f32[6,64]{1,0:T(8,128)}, f32[8,128]{1,0:T(8,128)}, f32[8,128]{1,0:T(8,128)}) custom-call(f32[32,4,128]{2,1,0:T(4,128)} %get-tuple-element.5.rx_hbm, f32[6,64]{1,0:T(8,128)} %get-tuple-element.6.fit_hbm, s32[8,8]{1,0:T(8,128)} %ht_hbm.3), custom_call_target="tpu_custom_call" | custom-call | tf_op jit(solution)/shard_map/pallas_call | solution.py:390
